TPU v7x, 512 devices: a whole 4x8x8 slice. The times are simulated.
512 devices in a mesh: row: 32 (over x, z), col: 16 (over y, core).
Axes of the slice: x: 4, y: 8, z: 8, core: 2. Of those that a mesh axis runs over, the one named last changes fastest.
Arguments:
- query_nope: bfloat16 [8, 128, 128], P(None, 'row'), may hold values from -9 to 9
- query_rope: bfloat16 [8, 128, 64], P(None, 'row'), may hold values from -10 to 80
- key_up_weight: bfloat16 [128, 128, 512], P('row'), may hold values from -0.5 to 0.5
- value_up_weight: bfloat16 [128, 512, 128], P('row'), may hold values from -0.25 to 0.25
- latent_cache: bfloat16 [2097152, 576], P(('row', 'col')), may hold values from -6 to 6
- lengths: int32 [8], replicated, may hold values from 1 to 262144, as said below
- page_table: int32 [8, 4096], replicated, may hold values from -1 to 32767, as said below
Outputs:
- head_values: bfloat16 [8, 16384], P(None, 'row')
Inputs may be any that keep to these rules, and one draw needn't show every extreme that they name: `lengths`: the largest length is exactly 262144. `page_table`: entry (r, p) is -1 exactly when p * 64 >= lengths[r]; all other entries are distinct cache pages, page k lying on the device of index k // 64 along row+col.
All inputs are finite; a program needn't handle non-finite values.
Results may differ from a plain program's by a relative error of at most 0.0094.
Values may be sent and summed in bfloat16 or wider, within the bound.
No kernel may reach another device: no remote copies, remote signals or barrier semaphores. Data moves between devices by JAX's collectives and lax.ppermute only.
A program may use at most 128 MiB of HBM per device.

v0:
```python
import jax
import jax.numpy as jnp
from jax import lax
from jax.sharding import PartitionSpec as P

HEAD_NOPE_WIDTH = 128
ROTARY_WIDTH = 64
PAGE = 64


MASKED = -1e30


def merged(array, axis, combine):
    everything = jax.tree.map(lambda part: lax.all_gather(part, axis), array)
    first = jax.tree.map(lambda part: part[0], everything)

    def merged_step(k, so_far):
        return combine(so_far, jax.tree.map(lambda part: part[k], everything))

    return lax.fori_loop(1, lax.axis_size(axis), merged_step, first)


def combine(first, second):
    top_first, denom_first, latent_first = first
    top_second, denom_second, latent_second = second
    top = jnp.maximum(top_first, top_second)
    weight_first = jnp.exp(top_first - top)
    weight_second = jnp.exp(top_second - top)
    denom = weight_first * denom_first + weight_second * denom_second
    latent_rows = weight_first[..., None] * latent_first + weight_second[..., None] * latent_second
    return (top, denom, latent_rows)


def fold_sources(top_parts, denom_parts, latent_parts):
    joint_top = jnp.max(top_parts, axis=0)
    source_weight = jnp.exp(top_parts - joint_top[None])
    joint_denom = jnp.sum(source_weight * denom_parts, axis=0)
    joint_latent = jnp.sum(source_weight[..., None] * latent_parts, axis=0)
    return (joint_top, joint_denom, joint_latent)


def local(
    query_nope, query_rope, key_up_weight, value_up_weight, latent_cache, lengths, page_table
):
    scale = float(HEAD_NOPE_WIDTH + ROTARY_WIDTH) ** (-0.5)
    requests, local_heads, _ = query_nope.shape
    kv_width = key_up_weight.shape[2]
    width = latent_cache.shape[1]
    query_latent = jnp.einsum(
        "rhn,hnc->rhc", query_nope, key_up_weight, preferred_element_type=jnp.float32
    ).astype(jnp.bfloat16)
    query = jnp.concatenate([query_latent, query_rope], axis=2)
    queries = lax.all_gather(query, "row", axis=1, tiled=True)
    heads = queries.shape[1]
    slots = latent_cache.shape[0] // PAGE
    table_width = page_table.shape[1]
    device = lax.axis_index("row") * lax.axis_size("col") + lax.axis_index("col")
    local_slot = page_table - device * slots
    matches = local_slot[:, :, None] == jnp.arange(slots, dtype=jnp.int32)[None, None, :]
    owned = jnp.any(matches, axis=1)
    page_index = jnp.sum(
        jnp.where(matches, jnp.arange(table_width, dtype=jnp.int32)[None, :, None], 0), axis=(0, 1)
    )
    limit = jnp.sum(jnp.where(owned, lengths[:, None], 0), axis=0)
    position = page_index[:, None] * PAGE + jnp.arange(PAGE, dtype=jnp.int32)[None, :]
    valid = position < limit[:, None]
    group = 8
    blocks = slots // group
    block_keys = latent_cache.reshape(blocks, group, PAGE, width)
    block_valid = valid.reshape(blocks, group, PAGE)
    block_owned = jnp.transpose(owned.reshape(requests, blocks, group), (1, 0, 2))

    def body_step(carry, items):
        top, denom, latent_rows = carry
        key_rows, live, owner = items
        slot_query = jnp.einsum(
            "rs,rhd->shd", owner.astype(jnp.bfloat16), queries, preferred_element_type=jnp.float32
        ).astype(jnp.bfloat16)
        scores = (
            jnp.einsum("shd,std->sht", slot_query, key_rows, preferred_element_type=jnp.float32)
            * scale
        )
        scores = jnp.where(live[:, None, :], scores, MASKED)
        slot_top = jnp.max(scores, axis=2)
        expo = jnp.where(live[:, None, :], jnp.exp(scores - slot_top[:, :, None]), 0.0).astype(
            jnp.bfloat16
        )
        slot_denom = jnp.sum(expo.astype(jnp.float32), axis=2)
        slot_latent = jnp.einsum(
            "sht,stc->shc", expo, key_rows[:, :, :kv_width], preferred_element_type=jnp.float32
        )
        candidate = jnp.where(owner[:, :, None], slot_top[None, :, :], MASKED)
        new_top = jnp.maximum(top, jnp.max(candidate, axis=1))
        keep = jnp.exp(top - new_top)
        weight = jnp.where(
            owner[:, :, None], jnp.exp(slot_top[None, :, :] - new_top[:, None, :]), 0.0
        )
        denom = denom * keep + jnp.sum(weight * slot_denom[None, :, :], axis=1)
        latent_rows = latent_rows * keep[..., None] + jnp.einsum(
            "rsh,shc->rhc", weight, slot_latent, precision=lax.Precision.HIGHEST
        )
        return ((new_top, denom, latent_rows), None)

    start_carry = (
        jnp.full((requests, heads), MASKED, jnp.float32),
        jnp.zeros((requests, heads), jnp.float32),
        jnp.zeros((requests, heads, kv_width), jnp.float32),
    )
    partials, _ = lax.scan(body_step, start_carry, (block_keys, block_valid, block_owned))
    sources = lax.axis_size("row")
    top_parts, denom_parts, latent_parts = (
        lax.all_to_all(partials[0], "row", split_axis=1, concat_axis=0, tiled=True),
        lax.all_to_all(partials[1], "row", split_axis=1, concat_axis=0, tiled=True),
        lax.all_to_all(partials[2], "row", split_axis=1, concat_axis=0, tiled=True),
    )
    row_part = fold_sources(
        top_parts.reshape(sources, requests, local_heads),
        denom_parts.reshape(sources, requests, local_heads),
        latent_parts.reshape(sources, requests, local_heads, kv_width),
    )
    _, denom, latent_rows = merged(row_part, "col", combine)
    attended = (latent_rows / denom[..., None]).astype(jnp.bfloat16)
    values = jnp.einsum(
        "rhc,hcv->rhv", attended, value_up_weight, preferred_element_type=jnp.float32
    )
    return values.astype(jnp.bfloat16).reshape(requests, local_heads * value_up_weight.shape[2])


def solution(mesh):
    placed = (
        P(None, "row", None),
        P(None, "row", None),
        P("row", None, None),
        P("row", None, None),
        P(("row", "col"), None),
        P(),
        P(),
    )
    return jax.shard_map(
        local, mesh=mesh, in_specs=placed, out_specs=P(None, "row"), check_vma=False
    )
```

profile of v0, /device:TPU:1, one launch (start us, length us, event | category | flops | bytes accessed | tf_op | source)
XLA Modules:
  0.0 333.3 jit_solution(6444400999808479567)
XLA Ops:
  6.5 0.8 copy.50
  7.6 0.9 fusion.28
  9.2 0.9 broadcast_subtract_fusion
  10.1 1.1 fusion.27
  11.3 0.7 select_reduce_fusion.2
  12.1 0.9 select_reduce_fusion.1
  13.2 7.7 %copy.51 = bf16[4096,576]{1,0:T(8,128)(2,1)} copy(bf16[4096,576]{0,1:T(8,128)(2,1)} %param.15) | data formatting | bytes 9437184 | tf_op args[4]
  20.9 73.7 %all-gather.8.cloned.1.call-done = bf16[8,128,576]{2,0,1:T(8,128)(2,1)} async-done(((bf16[8,4,576]{2,0,1:T(8,128)(2,1)}), bf16[8,128,576]{2,0,1:T(8,128)(2,1)}) %all-gather.8.cloned.1.call-update) | async-done | bytes 1179664 | tf_op jit(solution)/shard_map/all_gather | solution.py:54
  94.6 3.1 copy.53
  97.7 89.4 %while.35 = (s32[]{:T(128)}, f32[8,128]{0,1:T(8,128)S(1)}, f32[8,128]{0,1:T(8,128)S(1)}, f32[8,128,512]{2,0,1:T(8,128)}, pred[8,8,8]{2,1,0:T(8,128)(4,1)S(1)}, /...) while((s32[]{:T(128)}, f32[8,128]{0,1:T(8,128)S(1)}, ...), condition=%wide.region_8.9_spmd.clone, body=%wide.region_3.8_spmd.clone.sunk | while | flops 205327360 | bytes 15126977 | solution.py:110
  97.7 1.8 convolution_convert_fusion.4
  99.5 1.2 dynamic-slice_bitcast_fusion.6
  102.8 4.6 %bitcast_add_fusion.2 = f32[8,128,512]{2,0,1:T(8,128)} fusion(f32[8,128,512]{2,0,1:T(8,128)} %get-tuple-element.451, f32[8,128,512]{2,1,0:T(8,128)S(1)} %fusion.60, f32[8,128]{0,1:T(8,128)S(1)} %get-tuple-element.437, pred[]{:T(512)S(6)} %compare.3, f32[8,128]{0,1:T(8,128)S(1)} %select_maximum_fusion.2, f32[8,128]{0,1:T(8,128)S(1)} %copy.85, ...), kind=kOutput, calls=%fused_computation.8.clone.1 | convolution fusion | flops 51920896 | bytes 6303809 | tf_op jit(solution)/shard_map/while/body/eval_jaxpr/rsh,shc->rhc/dot_general | solution.py:100
  107.5 1.8 convolution_convert_fusion.4
  109.3 1.2 dynamic-slice_bitcast_fusion.6
  112.6 6.2 %bitcast_add_fusion.2 = f32[8,128,512]{2,0,1:T(8,128)} fusion(f32[8,128,512]{2,0,1:T(8,128)} %get-tuple-element.451, f32[8,128,512]{2,1,0:T(8,128)S(1)} %fusion.60, f32[8,128]{0,1:T(8,128)S(1)} %get-tuple-element.437, pred[]{:T(512)S(6)} %compare.3, f32[8,128]{0,1:T(8,128)S(1)} %select_maximum_fusion.2, f32[8,128]{0,1:T(8,128)S(1)} %copy.85, ...), kind=kOutput, calls=%fused_computation.8.clone.1 | convolution fusion | flops 51920896 | bytes 6303809 | tf_op jit(solution)/shard_map/while/body/eval_jaxpr/rsh,shc->rhc/dot_general | solution.py:100
  118.9 1.8 convolution_convert_fusion.4
  120.7 1.2 dynamic-slice_bitcast_fusion.6
  122.2 0.7 fusion.60
  124.0 6.2 %bitcast_add_fusion.2 = f32[8,128,512]{2,0,1:T(8,128)} fusion(f32[8,128,512]{2,0,1:T(8,128)} %get-tuple-element.451, f32[8,128,512]{2,1,0:T(8,128)S(1)} %fusion.60, f32[8,128]{0,1:T(8,128)S(1)} %get-tuple-element.437, pred[]{:T(512)S(6)} %compare.3, f32[8,128]{0,1:T(8,128)S(1)} %select_maximum_fusion.2, f32[8,128]{0,1:T(8,128)S(1)} %copy.85, ...), kind=kOutput, calls=%fused_computation.8.clone.1 | convolution fusion | flops 51920896 | bytes 6303809 | tf_op jit(solution)/shard_map/while/body/eval_jaxpr/rsh,shc->rhc/dot_general | solution.py:100
  130.2 1.8 convolution_convert_fusion.4
  132.0 1.2 dynamic-slice_bitcast_fusion.6
  133.6 0.7 fusion.60
  135.4 6.2 %bitcast_add_fusion.2 = f32[8,128,512]{2,0,1:T(8,128)} fusion(f32[8,128,512]{2,0,1:T(8,128)} %get-tuple-element.451, f32[8,128,512]{2,1,0:T(8,128)S(1)} %fusion.60, f32[8,128]{0,1:T(8,128)S(1)} %get-tuple-element.437, pred[]{:T(512)S(6)} %compare.3, f32[8,128]{0,1:T(8,128)S(1)} %select_maximum_fusion.2, f32[8,128]{0,1:T(8,128)S(1)} %copy.85, ...), kind=kOutput, calls=%fused_computation.8.clone.1 | convolution fusion | flops 51920896 | bytes 6303809 | tf_op jit(solution)/shard_map/while/body/eval_jaxpr/rsh,shc->rhc/dot_general | solution.py:100
  141.6 1.8 convolution_convert_fusion.4
  143.4 1.2 dynamic-slice_bitcast_fusion.6
  145.0 0.7 fusion.60
  146.7 6.2 %bitcast_add_fusion.2 = f32[8,128,512]{2,0,1:T(8,128)} fusion(f32[8,128,512]{2,0,1:T(8,128)} %get-tuple-element.451, f32[8,128,512]{2,1,0:T(8,128)S(1)} %fusion.60, f32[8,128]{0,1:T(8,128)S(1)} %get-tuple-element.437, pred[]{:T(512)S(6)} %compare.3, f32[8,128]{0,1:T(8,128)S(1)} %select_maximum_fusion.2, f32[8,128]{0,1:T(8,128)S(1)} %copy.85, ...), kind=kOutput, calls=%fused_computation.8.clone.1 | convolution fusion | flops 51920896 | bytes 6303809 | tf_op jit(solution)/shard_map/while/body/eval_jaxpr/rsh,shc->rhc/dot_general | solution.py:100
  153.0 1.8 convolution_convert_fusion.4
  154.8 1.2 dynamic-slice_bitcast_fusion.6
  156.4 0.7 fusion.60
  158.1 6.2 %bitcast_add_fusion.2 = f32[8,128,512]{2,0,1:T(8,128)} fusion(f32[8,128,512]{2,0,1:T(8,128)} %get-tuple-element.451, f32[8,128,512]{2,1,0:T(8,128)S(1)} %fusion.60, f32[8,128]{0,1:T(8,128)S(1)} %get-tuple-element.437, pred[]{:T(512)S(6)} %compare.3, f32[8,128]{0,1:T(8,128)S(1)} %select_maximum_fusion.2, f32[8,128]{0,1:T(8,128)S(1)} %copy.85, ...), kind=kOutput, calls=%fused_computation.8.clone.1 | convolution fusion | flops 51920896 | bytes 6303809 | tf_op jit(solution)/shard_map/while/body/eval_jaxpr/rsh,shc->rhc/dot_general | solution.py:100
  164.3 1.8 convolution_convert_fusion.4
  166.1 1.2 dynamic-slice_bitcast_fusion.6
  167.7 0.7 fusion.60
  169.5 6.2 %bitcast_add_fusion.2 = f32[8,128,512]{2,0,1:T(8,128)} fusion(f32[8,128,512]{2,0,1:T(8,128)} %get-tuple-element.451, f32[8,128,512]{2,1,0:T(8,128)S(1)} %fusion.60, f32[8,128]{0,1:T(8,128)S(1)} %get-tuple-element.437, pred[]{:T(512)S(6)} %compare.3, f32[8,128]{0,1:T(8,128)S(1)} %select_maximum_fusion.2, f32[8,128]{0,1:T(8,128)S(1)} %copy.85, ...), kind=kOutput, calls=%fused_computation.8.clone.1 | convolution fusion | flops 51920896 | bytes 6303809 | tf_op jit(solution)/shard_map/while/body/eval_jaxpr/rsh,shc->rhc/dot_general | solution.py:100
  175.7 1.8 convolution_convert_fusion.4
  177.5 1.2 dynamic-slice_bitcast_fusion.6
  180.8 6.2 %bitcast_add_fusion.2 = f32[8,128,512]{2,0,1:T(8,128)} fusion(f32[8,128,512]{2,0,1:T(8,128)} %get-tuple-element.451, f32[8,128,512]{2,1,0:T(8,128)S(1)} %fusion.60, f32[8,128]{0,1:T(8,128)S(1)} %get-tuple-element.437, pred[]{:T(512)S(6)} %compare.3, f32[8,128]{0,1:T(8,128)S(1)} %select_maximum_fusion.2, f32[8,128]{0,1:T(8,128)S(1)} %copy.85, ...), kind=kOutput, calls=%fused_computation.8.clone.1 | convolution fusion | flops 51920896 | bytes 6303809 | tf_op jit(solution)/shard_map/while/body/eval_jaxpr/rsh,shc->rhc/dot_general | solution.py:100
  187.1 14.3 %all_to_all.47 = f32[8,32,4]{0,2,1:T(4,128)S(1)} all-to-all(f32[8,32,4]{0,2,1:T(4,128)S(1)} %bitcast.81), channel_id=1, replica_groups=mesh['row'=32,'col'=16] {'row'}, dimensions={1} | all-to-all | bytes 8192 | tf_op jit(solution)/shard_map/all_to_all | solution.py:113
  201.3 11.8 %all_to_all.48 = f32[8,32,4]{0,2,1:T(4,128)S(1)} all-to-all(f32[8,32,4]{0,2,1:T(4,128)S(1)} %bitcast.82), channel_id=1, replica_groups=mesh['row'=32,'col'=16] {'row'}, dimensions={1} | all-to-all | bytes 8192 | tf_op jit(solution)/shard_map/all_to_all | solution.py:114
  213.1 4.0 %all-to-all-start.2 = ((f32[8,128,512]{2,0,1:T(8,128)}), f32[8,128,512]{2,0,1:T(8,128)S(1)}, u32[]{:S(2)}, u32[]{:S(2)}) async-start(f32[8,128,512]{2,0,1:T(8,128)} %get-tuple-element.228), calls=%async_computation.2 | async-start | bytes 4194304 | tf_op jit(solution)/shard_map/all_to_all | solution.py:115
  217.3 38.5 %all-to-all-done.2 = f32[8,128,512]{2,0,1:T(8,128)S(1)} async-done(((f32[8,128,512]{2,0,1:T(8,128)}), f32[8,128,512]{2,0,1:T(8,128)S(1)}, u32[]{:S(2)}, u32[]{:S(2)}) %all-to-all-start.2) | async-done | bytes 2097184 | tf_op jit(solution)/shard_map/all_to_all | solution.py:115
  256.7 30.1 %all-gather.4 = f32[16,8,4]{1,2,0:T(4,128)S(1)} all-gather(f32[1,8,4]{1,2,0:T(4,128)S(1)} %bitcast.86), channel_id=3, replica_groups=mesh['row'=32,'col'=16] {'col'}, dimensions={0}, use_global_device_ids=true | all-gather | bytes 2176 | tf_op jit(solution)/shard_map/all_gather | solution.py:15
  286.8 15.5 %all-gather.3 = f32[16,8,4]{1,2,0:T(4,128)S(1)} all-gather(f32[1,8,4]{1,2,0:T(4,128)S(1)} %bitcast.85), channel_id=2, replica_groups=mesh['row'=32,'col'=16] {'col'}, dimensions={0}, use_global_device_ids=true | all-gather | bytes 2176 | tf_op jit(solution)/shard_map/all_gather | solution.py:15
  302.3 5.0 %all-gather.10.cloned.1.call-done = f32[128,4,512]{2,1,0:T(4,128)} async-done(((f32[8,4,512]{2,1,0:T(4,128)}), f32[128,4,512]{2,1,0:T(4,128)}) %all-gather.10.cloned.1.call-update) | async-done | bytes 1048592 | tf_op jit(solution)/shard_map/all_gather | solution.py:15
  307.4 0.8 slice.24
  308.2 17.2 %while.34 = (s32[]{:T(128)}, f32[8,4]{0,1:T(4,128)S(1)}, f32[8,4]{0,1:T(4,128)S(1)}, f32[8,4,512]{2,1,0:T(4,128)S(1)}, f32[16,8,4]{1,2,0:T(4,128)S(1)}, /*index=...) while((s32[]{:T(128)}, f32[8,4]{0,1:T(4,128)S(1)}, ...), condition=%wide.region_13.14_spmd, body=%wide.region_12.13_spmd.sunk | while | flops 49349 | bytes 198551 | solution.py:21
  308.4 0.9 fusion.52
  309.5 0.9 fusion.52
  310.7 0.9 fusion.52
  311.8 0.9 fusion.52
  313.0 0.9 fusion.52
  314.1 0.9 fusion.52
  315.3 0.9 fusion.52
  316.4 0.9 fusion.52
  317.6 0.9 fusion.52
  318.7 0.9 fusion.52
  319.9 0.9 fusion.52
  321.0 0.9 fusion.52
  322.2 0.9 fusion.52
  323.3 0.9 fusion.52
  324.5 0.9 fusion.52
  325.6 0.8 fusion.29
  (162 shorter events, 18.7 us)
Async XLA Ops:
  6.5 1.1 copy-start
  6.5 88.1 %all-gather.8.cloned.1.call-start = ((), (), s32[]{:S(2)}) async-start(), calls=%async_computation.3 | async-start | bytes 1351680 | tf_op jit(solution)/shard_map/all_gather | solution.py:54
  213.1 42.6 %all-to-all-start.2 = ((f32[8,128,512]{2,0,1:T(8,128)}), f32[8,128,512]{2,0,1:T(8,128)S(1)}, u32[]{:S(2)}, u32[]{:S(2)}) async-start(f32[8,128,512]{2,0,1:T(8,128)} %get-tuple-element.228), calls=%async_computation.2 | async-start | bytes 4194304 | tf_op jit(solution)/shard_map/all_to_all | solution.py:115
  217.2 90.2 %all-gather.10.cloned.1.call-start = ((), (), s32[]{:S(2)}) async-start(), calls=%async_computation.4 | async-start | bytes 1114112 | tf_op jit(solution)/shard_map/all_gather | solution.py:15
  217.3 108.3 %copy-start.1 = (bf16[4,512,128]{2,1,0:T(8,128)(2,1)S(1)}, bf16[4,512,128]{2,1,0:T(8,128)(2,1)}, u32[]{:S(2)}) copy-start(bf16[4,512,128]{2,1,0:T(8,128)(2,1)} %param.14) | copy-start | bytes 1572868
Sparse Core Ops, SparseCore 0:
  10.5 84.0 all-gather.7
  256.8 50.5 all-gather.9
where the time goes:
time: 335 us; the launch traced here: 333 us
  waiting for transfers between devices  117 us (35%)
  matrix products  73.3 us (22%)
  blocking collectives  71.7 us (21%)
  local copies, waits for them, and re-layouts  27.1 us (8%)
  other arithmetic  25.5 us (8%)
  between operations  13.5 us (4%)
  starting transfers between devices  4.06 us (1%)
    all_gather x1, waiting for transfers between devices, local(): queries = lax.all_gather(query, 'row', axis=1, tiled=True)  73.7 us
    dot_general x8, matrix products, body_step(): jnp.einsum('rsh,shc->rhc', weight, slot_latent, precision=lax.Precision.H...  48.2 us
    all_gather x2, blocking collectives, merged(): everything = jax.tree.map(lambda part: lax.all_gather(part, axis), array)  45.6 us
    all_to_all x1, waiting for transfers between devices, local(): lax.all_to_all(partials[2], 'row', split_axis=1, concat_axis=0, tiled=True)  38.5 us
    dot_general x8, matrix products, body_step(): jnp.einsum('rs,rhd->shd', owner.astype(jnp.bfloat16), queries, preferred_...  14.3 us
    all_to_all x1, blocking collectives, local(): lax.all_to_all(partials[0], 'row', split_axis=1, concat_axis=0, tiled=True)  14.3 us
    add x15, other arithmetic, combine(): weight_first[..., None] * latent_first  14.1 us
    unnamed x8, local copies, waits for them, and re-layouts  11.8 us
  transfers between devices with their start and end apart: 3, of which 3 were waited for; matrix products, arithmetic and copies ran while one was open for 4% of the time, Pallas kernels for 0%

commit v1 on v0

v1 whole, which is shorter than its diff:
```python
import functools

import jax
import jax.numpy as jnp
from jax import lax
from jax.experimental import pallas as pl
from jax.experimental.pallas import tpu as pltpu
from jax.sharding import PartitionSpec as P

PAGE = 64
LANES = 128
EMPTY = -1e30
ENTRIES = 128
TRASH = 150
PLAN = 512
F32 = jnp.float32
BF16 = jnp.bfloat16
VMEM_LIMIT = 48 * 1024 * 1024


def three_terms(value):
    high = value.astype(BF16)
    rest = value - high.astype(F32)
    middle = rest.astype(BF16)
    low = (rest - middle.astype(F32)).astype(BF16)
    return high, middle, low


def stat_lanes(values, rows):
    lane = lax.broadcasted_iota(jnp.int32, (rows, LANES), 1)
    out = jnp.zeros((rows, LANES), F32)
    for head, value in enumerate(values):
        for at, term in enumerate(three_terms(value)):
            out = jnp.where(lane == 64 * head + at, term.astype(F32), out)
    return out


def read_stat(lanes, head):
    at = 64 * head
    return lanes[..., at : at + 1] + lanes[..., at + 1 : at + 2] + lanes[..., at + 2 : at + 3]


def query_kernel(core_ref, nope_ref, rope_ref, up_ref, out_ref):
    first = 2 * core_ref[0]
    copies = out_ref.shape[0]
    kv = up_ref.shape[2]
    parts, ropes = [], []
    for j in range(2):
        product = jnp.dot(nope_ref[first + j], up_ref[j], preferred_element_type=F32)
        parts.append(product.astype(BF16))
        ropes.append(rope_ref[first + j])
    row = jnp.concatenate(parts + ropes, axis=1)
    for k in range(copies):
        out_ref[k] = row


def plan_kernel(where_ref, length_ref, table_ref, plan_ref, vec, sm, count, fill, sem):
    base, core = where_ref[0], where_ref[1]
    requests, width = table_ref.shape
    page = lax.broadcasted_iota(jnp.int32, (1, width), 1)
    high = lax.broadcasted_iota(jnp.int32, (8, width), 0)
    low = lax.broadcasted_iota(jnp.int32, (16, width), 0)
    total = jnp.zeros((16, 16), F32)
    for r in range(requests):
        slot = table_ref[r : r + 1, :] - base
        live = jnp.clip(length_ref[r] - page * PAGE, 0, PAGE).astype(F32)
        hit = high == (slot >> 4)
        owner = jnp.where(hit, float(r + 1), 0.0)
        rows = jnp.where(hit, live, 0.0)
        left = jnp.concatenate([owner, rows], axis=0).astype(BF16)
        right = jnp.where(low == (slot & 15), 1.0, 0.0).astype(BF16)
        total = total + lax.dot_general(
            left, right, (((1,), (1,)), ((), ())), preferred_element_type=F32
        )
    vec[:, :16] = total.astype(jnp.int32)
    copy = pltpu.make_async_copy(vec, sm, sem)
    copy.start()
    copy.wait()

    def page_of(i, side):
        s = (2 * i + side + PAGE * core) & 127
        return sm[s >> 4, s & 15], sm[8 + (s >> 4), s & 15]

    for r in range(16):
        count[r] = 0

    @pl.loop(0, PLAN)
    def _(e):
        plan_ref[e] = 0

    @pl.loop(0, 64)
    def _(i):
        a, _ = page_of(i, 0)
        b, _ = page_of(i, 1)
        count[a] = count[a] + 1
        count[b] = count[b] + jnp.where(b == a, 0, 1)

    start = jnp.int32(0)
    fill[0] = TRASH
    for r in range(requests):
        fill[r + 1] = 2 * start
        groups = (count[r + 1] + 1) >> 1

        @pl.loop(start, start + groups)
        def _(g):
            plan_ref[8 + g] = r

        start = start + groups
    plan_ref[0] = start

    @pl.loop(0, 64)
    def _(i):
        a, rows_a = page_of(i, 0)
        b, rows_b = page_of(i, 1)
        at = fill[a]
        fill[a] = at + jnp.where(a > 0, 1, 0)
        plan_ref[ENTRIES + at] = i + (rows_a << 8) + (jnp.where(a == b, rows_b, 0) << 16)
        other = jnp.where(a == b, 0, b)
        at = fill[other]
        fill[other] = at + jnp.where(other > 0, 1, 0)
        plan_ref[ENTRIES + at] = i + (rows_b << 16)


def attention_kernel(
    scale, plan_ref, query_ref, own_ref, other_ref, out_ref, staged, query, scores, top, denom, total, cache, sems
):
    copies = [
        pltpu.make_async_copy(own_ref, cache.at[0], sems.at[0]),
        pltpu.make_async_copy(other_ref, cache.at[1], sems.at[1]),
    ]
    for copy in copies:
        copy.start()
    sources, requests, wide = query_ref.shape
    kv = total.shape[2]
    tiles = kv // LANES
    for t in range(wide // LANES):
        columns = query_ref[:, :, t * LANES : (t + 1) * LANES]
        staged[t] = columns.astype(F32).reshape(sources * requests, LANES)
    for r in range(requests):
        at = pl.ds(r, sources, stride=requests)
        for t in range(tiles):
            columns = slice(t * LANES, (t + 1) * LANES)
            query[r, :sources, columns] = staged[t, at, :].astype(BF16)
            query[r, sources:, columns] = staged[tiles + t, at, :].astype(BF16)
        rows = staged[2 * tiles, at, :].astype(BF16)
        query[r, :sources, kv:] = rows[:, :64]
        query[r, sources:, kv:] = rows[:, 64:]
    top[...] = jnp.full_like(top, EMPTY)
    denom[...] = jnp.zeros_like(denom)
    total[...] = jnp.zeros_like(total)
    for copy in copies:
        copy.wait()
    groups = plan_ref[0]
    lane = lax.broadcasted_iota(jnp.int32, (1, 2 * LANES), 1)
    within = lane & (PAGE - 1)

    def keys(g, depth):
        tiles = []
        for side in range(2):
            tile = plan_ref[ENTRIES + 2 * g + side] & 255
            at = pl.multiple_of((tile & 31) * LANES, LANES)
            tiles.append(cache[tile >> 5, :depth, pl.ds(at, LANES)])
        return jnp.concatenate(tiles, axis=1)

    @pl.loop(0, groups)
    def _(g):
        r = plan_ref[8 + g]
        first = plan_ref[ENTRIES + 2 * g]
        second = plan_ref[ENTRIES + 2 * g + 1]
        score = jnp.dot(query[r], keys(g, cache.shape[1]), preferred_element_type=F32)
        rows = jnp.where(
            lane < 2 * PAGE,
            jnp.where(lane < PAGE, (first >> 8) & 255, first >> 16),
            jnp.where(lane < 3 * PAGE, (second >> 8) & 255, second >> 16),
        )
        score = jnp.where(within < rows, score, EMPTY)
        scores[g] = score
        top[r] = jnp.maximum(top[r], jnp.maximum(score[:, :LANES], score[:, LANES:]))

    for r in range(requests):
        top[r] = jnp.broadcast_to(jnp.max(top[r], axis=1, keepdims=True), top.shape[1:])

    @pl.loop(0, groups)
    def _(g):
        r = plan_ref[8 + g]
        level = top[r]
        score = scores[g]
        expo = jnp.concatenate(
            [
                jnp.exp((score[:, :LANES] - level) * scale),
                jnp.exp((score[:, LANES:] - level) * scale),
            ],
            axis=1,
        ).astype(BF16)
        wide_expo = expo.astype(F32)
        denom[r] = denom[r] + wide_expo[:, :LANES] + wide_expo[:, LANES:]
        total[r] = total[r] + lax.dot_general(
            expo, keys(g, kv), (((1,), (1,)), ((), ())), preferred_element_type=F32
        )

    for r in range(requests):
        sums = jnp.sum(denom[r], axis=1, keepdims=True)
        some = sums > 0.0
        safe = jnp.where(some, sums, 1.0)
        level = jnp.where(some, top[r][:, :1] * scale + jnp.log(safe), EMPTY)
        rows = total[r] * (1.0 / safe)
        at = pl.ds(r, sources, stride=requests)
        for t in range(tiles):
            columns = slice(t * LANES, (t + 1) * LANES)
            staged[t, at, :] = rows[:sources, columns]
            staged[tiles + t, at, :] = rows[sources:, columns]
        staged[2 * tiles, at, :] = stat_lanes([level[:sources], level[sources:]], sources)
    for t in range(wide // LANES):
        columns = slice(t * LANES, (t + 1) * LANES)
        out_ref[:, :, columns] = staged[t].reshape(sources, requests, LANES).astype(BF16)


def fold_kernel(core_ref, part_ref, up_ref, out_ref):
    sources, requests, wide = part_ref.shape
    kv = up_ref.shape[1]
    stats = part_ref[:, :, 2 * kv :].astype(F32)
    outputs, levels = [], []
    for j in range(2):
        level = read_stat(stats, j)
        peak = jnp.max(level, axis=0)
        weight = jnp.exp(level - peak[None])
        norm = jnp.sum(weight, axis=0)
        rows = part_ref[:, :, j * kv : (j + 1) * kv].astype(F32)
        rows = jnp.sum(rows * weight, axis=0) / norm
        outputs.append(jnp.dot(rows.astype(BF16), up_ref[j], preferred_element_type=F32))
        levels.append(peak + jnp.log(norm))
    block = jnp.concatenate(outputs + [stat_lanes(levels, requests)], axis=1).astype(BF16)
    for k in range(out_ref.shape[0]):
        out_ref[k] = block


def merge_kernel(part_ref, out_ref):
    width = 2 * LANES
    both = part_ref[...].astype(F32)
    both = both.reshape(both.shape[0] // 2, 2, *both.shape[1:])
    for core in range(2):
        parts = both[:, core]
        stats = parts[:, :, width:]
        for j in range(2):
            level = read_stat(stats, j)
            weight = jnp.exp(level - jnp.max(level, axis=0)[None])
            rows = jnp.sum(parts[:, :, j * LANES : (j + 1) * LANES] * weight, axis=0)
            rows = rows / jnp.sum(weight, axis=0)
            at = (2 * core + j) * LANES
            out_ref[:, at : at + LANES] = rows.astype(BF16)


def vmem():
    return pl.BlockSpec(memory_space=pltpu.VMEM)


def smem():
    return pl.BlockSpec(memory_space=pltpu.SMEM)


def anywhere():
    return pl.BlockSpec(memory_space=pl.ANY)


def params():
    return pltpu.CompilerParams(vmem_limit_bytes=VMEM_LIMIT)


def make_queries(core, nope, rope, key_up, copies):
    heads, requests, width = nope.shape
    kv = key_up.shape[2]
    wide = 2 * kv + 2 * rope.shape[2]
    whole = lambda i, c: (0, 0, 0)
    return pl.pallas_call(
        query_kernel,
        grid_spec=pltpu.PrefetchScalarGridSpec(
            num_scalar_prefetch=1,
            grid=(1,),
            in_specs=[
                pl.BlockSpec(nope.shape, whole),
                pl.BlockSpec(rope.shape, whole),
                pl.BlockSpec((2, width, kv), lambda i, c: (c[0], 0, 0)),
            ],
            out_specs=pl.BlockSpec((copies, requests, wide), whole),
        ),
        out_shape=jax.ShapeDtypeStruct((copies, requests, wide), BF16),
        compiler_params=params(),
        name="queries",
    )(core, nope, rope, key_up)


def make_plan(where, lengths, table):
    return pl.pallas_call(
        plan_kernel,
        out_shape=jax.ShapeDtypeStruct((PLAN,), jnp.int32),
        in_specs=[smem(), smem(), vmem()],
        out_specs=smem(),
        scratch_shapes=[
            pltpu.VMEM((16, LANES), jnp.int32),
            pltpu.SMEM((16, LANES), jnp.int32),
            pltpu.SMEM((16,), jnp.int32),
            pltpu.SMEM((16,), jnp.int32),
            pltpu.SemaphoreType.DMA,
        ],
        compiler_params=params(),
        cost_estimate=pl.CostEstimate(flops=10_000_000, bytes_accessed=4_000_000, transcendentals=0),
        name="plan",
    )(where, lengths, table)


def attend(scale, plan, queries, own, other):
    sources, requests, wide = queries.shape
    width, tokens = own.shape
    kv = (wide - 128) // 2
    heads = 2 * sources
    return pl.pallas_call(
        functools.partial(attention_kernel, scale),
        out_shape=jax.ShapeDtypeStruct((sources, requests, wide), BF16),
        in_specs=[smem(), vmem(), anywhere(), anywhere()],
        out_specs=vmem(),
        scratch_shapes=[
            pltpu.VMEM((wide // LANES, sources * requests, LANES), F32),
            pltpu.VMEM((requests, heads, width), BF16),
            pltpu.VMEM((72, heads, 2 * LANES), F32),
            pltpu.VMEM((requests, heads, LANES), F32),
            pltpu.VMEM((requests, heads, LANES), F32),
            pltpu.VMEM((requests, heads, kv), F32),
            pltpu.VMEM((2, width, tokens), BF16),
            pltpu.SemaphoreType.DMA((2,)),
        ],
        compiler_params=params(),
        cost_estimate=pl.CostEstimate(
            flops=1_200_000_000, bytes_accessed=12_000_000, transcendentals=524_288
        ),
        name="attention",
    )(plan, queries, own, other)


def fold(core, parts, value_up, copies):
    sources, requests, wide = parts.shape
    kv, out = value_up.shape[1:]
    whole = lambda i, c: (0, 0, 0)
    return pl.pallas_call(
        fold_kernel,
        grid_spec=pltpu.PrefetchScalarGridSpec(
            num_scalar_prefetch=1,
            grid=(1,),
            in_specs=[
                pl.BlockSpec(parts.shape, whole),
                pl.BlockSpec((2, kv, out), lambda i, c: (c[0], 0, 0)),
            ],
            out_specs=pl.BlockSpec((copies, requests, 3 * LANES), whole),
        ),
        out_shape=jax.ShapeDtypeStruct((copies, requests, 3 * LANES), BF16),
        compiler_params=params(),
        name="fold",
    )(core, parts, value_up)


def merge(parts):
    requests = parts.shape[1]
    return pl.pallas_call(
        merge_kernel,
        out_shape=jax.ShapeDtypeStruct((requests, 4 * LANES), BF16),
        in_specs=[vmem()],
        out_specs=vmem(),
        compiler_params=params(),
        name="merge",
    )(parts)


def local(query_nope, query_rope, key_up, value_up, cache, lengths, table):
    scale = float(query_nope.shape[2] + query_rope.shape[2]) ** -0.5
    rows, cols = lax.axis_size("row"), lax.axis_size("col")
    column = lax.axis_index("col")
    core = (column % 2).astype(jnp.int32)
    chip = lax.axis_index("row") * (cols // 2) + column // 2
    own = cache.T
    swap = [(i, i ^ 1) for i in range(cols)]
    other = lax.ppermute(own, "col", swap)
    queries = make_queries(
        core[None], jnp.swapaxes(query_nope, 0, 1), jnp.swapaxes(query_rope, 0, 1), key_up, rows
    )
    queries = lax.all_to_all(queries, "row", split_axis=0, concat_axis=0, tiled=True)
    where = jnp.stack([chip * 128, core]).astype(jnp.int32)
    plan = make_plan(where, lengths, table)
    parts = attend(scale, plan, queries, own, other)
    parts = lax.all_to_all(parts, "row", split_axis=0, concat_axis=0, tiled=True)
    parts = fold(core[None], parts, value_up, cols)
    parts = lax.all_to_all(parts, "col", split_axis=0, concat_axis=0, tiled=True)
    return merge(parts)


def solution(mesh):
    placed = (
        P(None, "row", None),
        P(None, "row", None),
        P("row", None, None),
        P("row", None, None),
        P(("row", "col"), None),
        P(),
        P(),
    )
    return jax.shard_map(
        local, mesh=mesh, in_specs=placed, out_specs=P(None, "row"), check_vma=False
    )
```

time: 335 us -> 99.8 us (0.30)
  waiting for transfers between devices: 117 us -> 5.81 us
  matrix products: 73.3 us -> 0 us
  blocking collectives: 71.7 us -> 43.1 us
  Pallas kernels: 0 us -> 27.6 us
  other arithmetic: 25.5 us -> 0.08 us
  local copies, waits for them, and re-layouts: 27.1 us -> 6.34 us
  between operations: 13.5 us -> 0.07 us
  starting transfers between devices: 4.06 us -> 16.3 us
    all_gather x2 -> x0, waiting for transfers between devices: 78.7 us -> none  [the longest x1 73.7 us: local(): queries = lax.all_gather(query, 'row', axis=1, tiled=True)]
    dot_general x34 -> x0, matrix products: 73.3 us -> none  [the longest x8 48.2 us: body_step(): jnp.einsum('rsh,shc->rhc', weight, slot_latent, precision=lax.Precision.H...]
    all_gather x2 -> x0, blocking collectives: 45.6 us -> none  [merged(): everything = jax.tree.map(lambda part: lax.all_gather(part, axis), array)]
    all_to_all x1, waiting for transfers between devices: 38.5 us -> 5.8 us  [local(): lax.all_to_all(queries, 'row', split_axis=0, concat_axis=0, tiled=True)]
    pallas_call x0 -> x5, Pallas kernels: none -> 27.6 us  [the longest x1 17 us: attend(): pl.pallas_call(functools.partial(attention_kernel, scale), out_shape=jax....]
    all_to_all x2, blocking collectives: 26.1 us -> 43.1 us  [the longest x1 21.8 us: local(): lax.all_to_all(parts, 'col', split_axis=0, concat_axis=0, tiled=True)]
    add x38 -> x0, other arithmetic: 14.8 us -> none  [the longest x15 14.1 us: combine(): weight_first[..., None] * latent_first]
    squeeze x8 -> x0, local copies, waits for them, and re-layouts: 9.21 us -> none  [local(): lax.scan(body_step, start_carry, (block_keys, block_valid, block_owned))]
  transfers between devices with their start and end apart: 3 -> 2, of which waited for: 3 -> 1; matrix products, arithmetic and copies ran while one was open for 4% -> 1% of each run, Pallas kernels for 0% -> 9%
where the time goes in v1:
time: 99.8 us; the launch traced here: 99.3 us
  blocking collectives  43.1 us (43%)
  Pallas kernels  27.6 us (28%)
  starting transfers between devices  16.3 us (16%)
  local copies, waits for them, and re-layouts  6.34 us (6%)
  waiting for transfers between devices  5.81 us (6%)
    all_to_all x1, blocking collectives, local(): lax.all_to_all(parts, 'col', split_axis=0, concat_axis=0, tiled=True)  21.8 us
    all_to_all x1, blocking collectives, local(): lax.all_to_all(parts, 'row', split_axis=0, concat_axis=0, tiled=True)  21.3 us
    pallas_call x1, Pallas kernels, attend(): pl.pallas_call(functools.partial(attention_kernel, scale), out_shape=jax....  17 us
    ppermute x1, starting transfers between devices, local(): other = lax.ppermute(own, 'col', swap)  8.78 us
    pallas_call x1, Pallas kernels, make_plan(): pl.pallas_call(plan_kernel, out_shape=jax.ShapeDtypeStruct((PLAN,), jnp.i...  8.38 us
    all_to_all x1, starting transfers between devices, local(): lax.all_to_all(queries, 'row', split_axis=0, concat_axis=0, tiled=True)  7.51 us
    unnamed x12, local copies, waits for them, and re-layouts  6.34 us
    all_to_all x1, waiting for transfers between devices, local(): lax.all_to_all(queries, 'row', split_axis=0, concat_axis=0, tiled=True)  5.8 us
  transfers between devices with their start and end apart: 2, of which 1 were waited for; matrix products, arithmetic and copies ran while one was open for 1% of the time, Pallas kernels for 9%

profile of v1, /device:TPU:1, one launch (start us, length us, event | category | flops | bytes accessed | tf_op | source)
XLA Modules:
  0.0 99.3 jit_solution(4688878590756320519)
XLA Ops:
  0.0 8.8 %collective-permute-start = (bf16[576,4096]{1,0:T(8,128)(2,1)}, bf16[576,4096]{1,0:T(8,128)(2,1)}, u32[]{:S(2)}, u32[]{:S(2)}) collective-permute-start(bf16[576,4096]{1,0:T(8,128)(2,1)} %bitcast.9), channel_id=1, source_target_pairs={{0,1},{1,0},{2,3},{3,2},{4,5},{5,4},{6,7},{7,6},{8,9},{9,8},{10,11... | collective-permute-start | bytes 14155784 | tf_op jit(solution)/shard_map/ppermute | solution.py:380
  8.8 0.7 copy.13
  9.5 0.7 copy.12
  10.2 0.0 copy-start.1
  10.2 1.0 %copy-done.1 = bf16[4,128,512]{2,1,0:T(8,128)(2,1)S(1)} copy-done((bf16[4,128,512]{2,1,0:T(8,128)(2,1)S(1)}, bf16[4,128,512]{2,1,0:T(8,128)(2,1)}, u32[]{:S(2)}) %copy-start.1) | copy-done | bytes 524312
  11.2 1.0 %queries.1 = bf16[32,8,1152]{2,1,0:T(8,128)(2,1)} custom-call(s32[1]{0:T(128)} %bitcast.core_ref, bf16[4,8,128]{2,1,0:T(8,128)(2,1)S(1)} %bitcast.11, bf16[4,8,64]{2,1,0:T(8,128)(2,1)S(1)} %bitcast.12, bf16[4,128,512]{2,1,0:T(8,128)(2,1)S(1)} %copy-done.1), custom_call_target="tpu_custom_call" | custom-call | tf_op jit(solution)/shard_map/queries/pallas_call | solution.py:274
  12.2 7.5 %all-to-all-start = ((bf16[32,8,1152]{2,1,0:T(8,128)(2,1)}), bf16[32,8,1152]{2,1,0:T(8,128)(2,1)S(1)}, u32[]{:S(2)}, u32[]{:S(2)}) async-start(bf16[32,8,1152]{2,1,0:T(8,128)(2,1)} %queries.1), calls=%async_computation | async-start | bytes 1179648 | tf_op jit(solution)/shard_map/all_to_all | solution.py:384
  19.8 0.1 pad_add_fusion.where_ref
  19.9 0.0 copy-start.3
  19.9 0.9 copy-done.3
  20.8 0.0 copy-start.4
  20.8 0.7 copy-done.4
  21.4 8.4 %plan.1.plan_ref = s32[512]{0:T(512)S(1)} custom-call(s32[2]{0:T(128)S(1)} %pad_add_fusion.where_ref, s32[8]{0:T(128)S(1)} %copy-done.4, s32[8,4096]{1,0:T(8,128)S(1)} %copy-done.3), custom_call_target="tpu_custom_call" | custom-call | flops 10000000 | bytes 4000000 | tf_op jit(solution)/shard_map/plan/pallas_call | solution.py:293
  29.8 5.8 %all-to-all-done.query_ref = bf16[32,8,1152]{2,1,0:T(8,128)(2,1)S(1)} async-done(((bf16[32,8,1152]{2,1,0:T(8,128)(2,1)}), bf16[32,8,1152]{2,1,0:T(8,128)(2,1)S(1)}, u32[]{:S(2)}, u32[]{:S(2)}) %all-to-all-start) | async-done | bytes 589856 | tf_op jit(solution)/shard_map/all_to_all | solution.py:384
  35.6 0.0 collective-permute-done.other_ref
  35.6 0.0 copy-start
  35.6 2.3 %copy-done = bf16[4096,576]{0,1:T(8,128)(2,1)S(1)} copy-done((bf16[4096,576]{0,1:T(8,128)(2,1)S(1)}, bf16[4096,576]{0,1:T(8,128)(2,1)}, u32[]{:S(2)}) %copy-start) | copy-done | bytes 4718616
  38.0 0.0 copy-start.2
  38.0 17.0 %attention.1 = bf16[32,8,1152]{2,1,0:T(8,128)(2,1)S(1)} custom-call(s32[512]{0:T(512)S(1)} %plan.1.plan_ref, bf16[32,8,1152]{2,1,0:T(8,128)(2,1)S(1)} %all-to-all-done.query_ref, bf16[576,4096]{1,0:T(8,128)(2,1)S(1)} %bitcast.10, bf16[576,4096]{1,0:T(8,128)(2,1)} %collective-permute-done.other_ref), custom_call_target="tpu_custom_call" | custom-call | flops 1200000000 | bytes 12000000 | tf_op jit(solution)/shard_map/attention/pallas_call | solution.py:316
  55.0 21.3 %all_to_all.15.part_ref = bf16[32,8,1152]{2,1,0:T(8,128)(2,1)S(1)} all-to-all(bf16[32,8,1152]{2,1,0:T(8,128)(2,1)S(1)} %attention.1), channel_id=1, replica_groups=mesh['row'=32,'col'=16] {'row'}, dimensions={0} | all-to-all | bytes 1179648 | tf_op jit(solution)/shard_map/all_to_all | solution.py:388
  76.3 0.0 copy-done.2
  76.3 0.4 fold.1
  76.7 21.8 %all_to_all.16.part_ref = bf16[16,8,384]{2,1,0:T(8,128)(2,1)S(1)} all-to-all(bf16[16,8,384]{2,1,0:T(8,128)(2,1)S(1)} %fold.1), channel_id=1, replica_groups=mesh['row'=32,'col'=16] {'col'}, dimensions={0} | all-to-all | bytes 196608 | tf_op jit(solution)/shard_map/all_to_all | solution.py:390
  98.5 0.8 merge.1
Async XLA Ops:
  0.0 35.6 %collective-permute-start = (bf16[576,4096]{1,0:T(8,128)(2,1)}, bf16[576,4096]{1,0:T(8,128)(2,1)}, u32[]{:S(2)}, u32[]{:S(2)}) collective-permute-start(bf16[576,4096]{1,0:T(8,128)(2,1)} %bitcast.9), channel_id=1, source_target_pairs={{0,1},{1,0},{2,3},{3,2},{4,5},{5,4},{6,7},{7,6},{8,9},{9,8},{10,11... | collective-permute-start | bytes 14155784 | tf_op jit(solution)/shard_map/ppermute | solution.py:380
  10.2 1.0 %copy-start.1 = (bf16[4,128,512]{2,1,0:T(8,128)(2,1)S(1)}, bf16[4,128,512]{2,1,0:T(8,128)(2,1)}, u32[]{:S(2)}) copy-start(bf16[4,128,512]{2,1,0:T(8,128)(2,1)} %up_ref.2) | copy-start | bytes 1572868
  12.2 23.4 %all-to-all-start = ((bf16[32,8,1152]{2,1,0:T(8,128)(2,1)}), bf16[32,8,1152]{2,1,0:T(8,128)(2,1)S(1)}, u32[]{:S(2)}, u32[]{:S(2)}) async-start(bf16[32,8,1152]{2,1,0:T(8,128)(2,1)} %queries.1), calls=%async_computation | async-start | bytes 1179648 | tf_op jit(solution)/shard_map/all_to_all | solution.py:384
  19.9 0.9 copy-start.3
  20.8 0.7 copy-start.4
  35.6 2.3 %copy-start = (bf16[4096,576]{0,1:T(8,128)(2,1)S(1)}, bf16[4096,576]{0,1:T(8,128)(2,1)}, u32[]{:S(2)}) copy-start(bf16[4096,576]{0,1:T(8,128)(2,1)} %param.11) | copy-start | bytes 14155780
  38.0 38.4 %copy-start.2 = (bf16[4,512,128]{2,1,0:T(8,128)(2,1)S(1)}, bf16[4,512,128]{2,1,0:T(8,128)(2,1)}, u32[]{:S(2)}) copy-start(bf16[4,512,128]{2,1,0:T(8,128)(2,1)} %up_ref.3) | copy-start | bytes 1572868

commit v2 on v1

v2 whole, which is shorter than its diff:
```python
import functools

import jax
import jax.numpy as jnp
from jax import lax
from jax.experimental import pallas as pl
from jax.experimental.pallas import tpu as pltpu
from jax.sharding import PartitionSpec as P

PAGE = 64
LANES = 128
EMPTY = -1e30
UNROLL = 4
GROUPS = 40
STEPS = GROUPS // UNROLL
CHUNK = UNROLL * 2 * LANES
MIB = 1024 * 1024
ALL_VMEM = 40 * MIB
ENTRIES = 64
TRASH = 180
PLAN = 256
F32 = jnp.float32
BF16 = jnp.bfloat16


def three_terms(value):
    high = value.astype(BF16)
    rest = value - high.astype(F32)
    middle = rest.astype(BF16)
    low = (rest - middle.astype(F32)).astype(BF16)
    return high, middle, low


def stat_lanes(values, rows):
    lane = lax.broadcasted_iota(jnp.int32, (rows, LANES), 1)
    out = jnp.zeros((rows, LANES), F32)
    for head, value in enumerate(values):
        for at, term in enumerate(three_terms(value)):
            out = jnp.where(lane == 64 * head + at, term.astype(F32), out)
    return out


def read_stat(lanes, head):
    at = 64 * head
    return lanes[..., at : at + 1] + lanes[..., at + 1 : at + 2] + lanes[..., at + 2 : at + 3]


def query_kernel(nope_any, rope_any, up_ref, out_ref, nope_ref, rope_ref, up, row, sems, out_sems):
    copies, requests, _ = out_ref.shape
    first = 2 * (lax.axis_index("col") & 1)
    loads = [
        pltpu.make_async_copy(nope_any, nope_ref, sems.at[0]),
        pltpu.make_async_copy(rope_any, rope_ref, sems.at[1]),
        pltpu.make_async_copy(up_ref.at[pl.ds(first, 2)], up, sems.at[2]),
    ]
    for load in loads:
        load.start()

    def head_of(ref, j):
        rows = ref[...].astype(F32)
        head = lax.broadcasted_iota(jnp.int32, rows.shape, 1)
        return jnp.sum(jnp.where(head == first + j, rows, 0.0), axis=1).astype(BF16)

    loads[0].wait()
    nopes = [head_of(nope_ref, j) for j in range(2)]
    loads[1].wait()
    ropes = [head_of(rope_ref, j) for j in range(2)]
    loads[2].wait()
    parts = [
        jnp.dot(nopes[j], up[j], preferred_element_type=F32).astype(BF16) for j in range(2)
    ]
    row[...] = jnp.concatenate(parts + ropes, axis=1)
    stores = [
        pltpu.make_async_copy(row, out_ref.at[k], out_sems.at[k]) for k in range(copies)
    ]
    for store in stores:
        store.start()
    for store in stores:
        store.wait()


def gather_kernel(
    length_ref,
    table_any,
    own_ref,
    other_ref,
    plan_ref,
    keys_ref,
    table_ref,
    cache,
    keys,
    vec,
    sm,
    count,
    fill,
    sem,
    cache_sems,
    out_sems,
):
    loads = [
        pltpu.make_async_copy(own_ref, cache.at[0], cache_sems.at[0]),
        pltpu.make_async_copy(other_ref, cache.at[1], cache_sems.at[1]),
    ]
    copy = pltpu.make_async_copy(table_any, table_ref, sem)
    copy.start()
    for load in loads:
        load.start()
    copy.wait()
    column = lax.axis_index("col")
    core = column & 1
    chip = lax.axis_index("row") * (lax.axis_size("col") // 2) + (column >> 1)
    base = chip * 128
    requests, width = table_ref.shape
    page = lax.broadcasted_iota(jnp.int32, (1, width), 1)
    high = lax.broadcasted_iota(jnp.int32, (8, width), 0)
    low = lax.broadcasted_iota(jnp.int32, (16, width), 0)
    total = jnp.zeros((16, 16), F32)
    for r in range(requests):
        slot = table_ref[r : r + 1, :] - base
        live = jnp.clip(length_ref[r] - page * PAGE, 0, PAGE).astype(F32)
        hit = high == (slot >> 4)
        owner = jnp.where(hit, float(r + 1), 0.0)
        rows = jnp.where(hit, live, 0.0)
        left = jnp.concatenate([owner, rows], axis=0).astype(BF16)
        right = jnp.where(low == (slot & 15), 1.0, 0.0).astype(BF16)
        total = total + lax.dot_general(
            left, right, (((1,), (1,)), ((), ())), preferred_element_type=F32
        )
    vec[:, :16] = total.astype(jnp.int32)
    copy = pltpu.make_async_copy(vec, sm, sem)
    copy.start()
    copy.wait()

    def page_of(i, side):
        s = (2 * i + side + PAGE * core) & 127
        return sm[s >> 4, s & 15], sm[8 + (s >> 4), s & 15]

    for r in range(16):
        count[r] = 0

    def page_of(t):
        s = (t + PAGE * core) & 127
        return sm[s >> 4, s & 15], sm[8 + (s >> 4), s & 15]

    @pl.loop(0, 128, unroll=16)
    def _(t):
        owner, _ = page_of(t)
        count[owner] = count[owner] + 1

    start = jnp.int32(0)
    fill[0] = TRASH
    for r in range(requests):
        fill[r + 1] = 4 * start
        groups = (count[r + 1] + 3) >> 2

        @pl.loop(start, start + groups)
        def _(g):
            plan_ref[8 + g] = r
            for at in range(4):
                plan_ref[ENTRIES + 4 * g + at] = 0

        start = start + groups
    plan_ref[0] = start
    for ahead in range(UNROLL - 1):
        plan_ref[8 + start + ahead] = 0
        for at in range(4):
            plan_ref[ENTRIES + 4 * (start + ahead) + at] = 0

    @pl.loop(0, 128, unroll=8)
    def _(t):
        owner, rows = page_of(t)
        at = fill[owner]
        fill[owner] = at + jnp.where(owner > 0, 1, 0)
        plan_ref[ENTRIES + at] = t + (rows << 8)

    for load in loads:
        load.wait()
    steps = (plan_ref[0] + UNROLL - 1) // UNROLL
    left_half = lax.broadcasted_iota(jnp.int32, (1, LANES), 1) < PAGE

    def tile_of(entry):
        slot = entry & 127
        at = pl.multiple_of(((slot & 63) >> 1) * LANES, LANES)
        return cache[slot >> 6, :, pl.ds(at, LANES)]

    def turned(tile):
        return jnp.concatenate([tile[:, PAGE:], tile[:, :PAGE]], axis=1)

    def chunk(step):
        at = pl.ds(pl.multiple_of(step * CHUNK, CHUNK), CHUNK)
        return pltpu.make_async_copy(keys.at[:, at], keys_ref.at[:, at], out_sems.at[step])

    @pl.loop(0, steps)
    def _(step):
        @pl.loop(step * 2 * UNROLL, (step + 1) * 2 * UNROLL)
        def _(j):
            first = plan_ref[ENTRIES + 2 * j]
            second = plan_ref[ENTRIES + 2 * j + 1]
            kind = (first & 1) + 2 * (second & 1)
            at = pl.ds(pl.multiple_of(j * LANES, LANES), LANES)

            @pl.when(kind == 2)
            def _():
                keys[:, at] = jnp.where(left_half, tile_of(first), tile_of(second))

            @pl.when(kind == 0)
            def _():
                keys[:, at] = jnp.where(left_half, tile_of(first), turned(tile_of(second)))

            @pl.when(kind == 3)
            def _():
                keys[:, at] = jnp.where(left_half, turned(tile_of(first)), tile_of(second))

            @pl.when(kind == 1)
            def _():
                keys[:, at] = turned(jnp.where(left_half, tile_of(second), tile_of(first)))

        chunk(step).start()

    @pl.loop(0, steps)
    def _(step):
        chunk(step).wait()


def attention_kernel(
    scale, plan_ref, query_any, keys_any, out_ref, query_ref, query_sem, staged, query, scores, top, denom, total, keys_ref, sems
):
    load = pltpu.make_async_copy(query_any, query_ref, query_sem)
    load.start()
    groups = plan_ref[0]
    steps = (groups + UNROLL - 1) // UNROLL

    def chunk(step):
        at = pl.ds(pl.multiple_of(step * CHUNK, CHUNK), CHUNK)
        return pltpu.make_async_copy(keys_any.at[:, at], keys_ref.at[:, at], sems.at[step])

    @pl.loop(0, steps)
    def _(step):
        chunk(step).start()

    sources, requests, wide = query_ref.shape
    kv = total.shape[2]
    tiles = kv // LANES
    top[...] = jnp.full_like(top, EMPTY)
    denom[...] = jnp.zeros_like(denom)
    total[...] = jnp.zeros_like(total)
    load.wait()
    for t in range(wide // LANES):
        columns = query_ref[:, :, t * LANES : (t + 1) * LANES]
        staged[t] = columns.astype(F32).reshape(sources * requests, LANES)
    for r in range(requests):
        at = pl.ds(r, sources, stride=requests)
        for t in range(tiles):
            columns = slice(t * LANES, (t + 1) * LANES)
            query[r, :sources, columns] = staged[t, at, :].astype(BF16)
            query[r, sources:, columns] = staged[tiles + t, at, :].astype(BF16)
        rows = staged[2 * tiles, at, :].astype(BF16)
        query[r, :sources, kv:] = rows[:, :64]
        query[r, sources:, kv:] = rows[:, 64:]
    lane = lax.broadcasted_iota(jnp.int32, (1, LANES), 1)
    left_half = lane < PAGE
    within = lane & (PAGE - 1)

    def keys(g, depth):
        return keys_ref[:depth, pl.ds(pl.multiple_of(g * 2 * LANES, 2 * LANES), 2 * LANES)]

    @pl.loop(0, steps)
    def _(step):
        chunk(step).wait()
        for u in range(UNROLL):
            g = step * UNROLL + u
            r = plan_ref[8 + g]
            score = jnp.dot(query[r], keys(g, keys_ref.shape[0]), preferred_element_type=F32)
            halves = []
            for half in range(2):
                rows = jnp.where(
                    left_half,
                    plan_ref[ENTRIES + 4 * g + 2 * half] >> 8,
                    plan_ref[ENTRIES + 4 * g + 2 * half + 1] >> 8,
                )
                part = score[:, half * LANES : (half + 1) * LANES]
                part = jnp.where(within < rows, part, EMPTY)
                scores[g, :, half * LANES : (half + 1) * LANES] = part
                halves.append(part)
            top[r] = jnp.maximum(top[r], jnp.maximum(*halves))

    for r in range(requests):
        top[r] = jnp.broadcast_to(jnp.max(top[r], axis=1, keepdims=True), top.shape[1:])

    @pl.loop(0, steps)
    def _(step):
        for u in range(UNROLL):
            g = step * UNROLL + u
            r = plan_ref[8 + g]
            level = top[r]
            live = jnp.where(g < groups, 1.0, 0.0)
            halves = []
            for half in range(2):
                part = scores[g, :, half * LANES : (half + 1) * LANES]
                halves.append((jnp.exp((part - level) * scale) * live).astype(BF16))
            denom[r] = denom[r] + halves[0].astype(F32) + halves[1].astype(F32)
            total[r] = total[r] + lax.dot_general(
                jnp.concatenate(halves, axis=1),
                keys(g, kv),
                (((1,), (1,)), ((), ())),
                preferred_element_type=F32,
            )

    for r in range(requests):
        sums = jnp.sum(denom[r], axis=1, keepdims=True)
        some = sums > 0.0
        safe = jnp.where(some, sums, 1.0)
        level = jnp.where(some, top[r][:, :1] * scale + jnp.log(safe), EMPTY)
        rows = total[r] * (1.0 / safe)
        at = pl.ds(r, sources, stride=requests)
        for t in range(tiles):
            columns = slice(t * LANES, (t + 1) * LANES)
            staged[t, at, :] = rows[:sources, columns]
            staged[tiles + t, at, :] = rows[sources:, columns]
        staged[2 * tiles, at, :] = stat_lanes([level[:sources], level[sources:]], sources)
    for t in range(wide // LANES):
        columns = slice(t * LANES, (t + 1) * LANES)
        out_ref[:, :, columns] = staged[t].reshape(sources, requests, LANES).astype(BF16)


def fold_kernel(part_ref, up_any, out_ref, up_ref, sem):
    first = 2 * (lax.axis_index("col") & 1)
    load = pltpu.make_async_copy(up_any.at[pl.ds(first, 2)], up_ref, sem)
    load.start()
    sources, requests, wide = part_ref.shape
    kv = up_ref.shape[1]
    stats = part_ref[:, :, 2 * kv :].astype(F32)
    outputs, levels = [], []
    for j in range(2):
        level = read_stat(stats, j)
        peak = jnp.max(level, axis=0)
        weight = jnp.exp(level - peak[None])
        norm = jnp.sum(weight, axis=0)
        rows = part_ref[:, :, j * kv : (j + 1) * kv].astype(F32)
        rows = jnp.sum(rows * weight, axis=0) / norm
        if j == 0:
            load.wait()
        outputs.append(jnp.dot(rows.astype(BF16), up_ref[j], preferred_element_type=F32))
        levels.append(peak + jnp.log(norm))
    block = jnp.concatenate(outputs + [stat_lanes(levels, requests)], axis=1).astype(BF16)
    for k in range(out_ref.shape[0]):
        out_ref[k] = block


def merge_kernel(part_ref, out_ref):
    width = 2 * LANES
    both = part_ref[...].astype(F32)
    both = both.reshape(both.shape[0] // 2, 2, *both.shape[1:])
    for core in range(2):
        parts = both[:, core]
        stats = parts[:, :, width:]
        for j in range(2):
            level = read_stat(stats, j)
            weight = jnp.exp(level - jnp.max(level, axis=0)[None])
            rows = jnp.sum(parts[:, :, j * LANES : (j + 1) * LANES] * weight, axis=0)
            rows = rows / jnp.sum(weight, axis=0)
            at = (2 * core + j) * LANES
            out_ref[:, at : at + LANES] = rows.astype(BF16)


def vmem():
    return pl.BlockSpec(memory_space=pltpu.VMEM)


def smem():
    return pl.BlockSpec(memory_space=pltpu.SMEM)


def anywhere():
    return pl.BlockSpec(memory_space=pl.ANY)


def params(limit=32 * MIB):
    return pltpu.CompilerParams(vmem_limit_bytes=limit)


def make_queries(nope, rope, key_up, copies):
    requests, heads, width = nope.shape
    kv = key_up.shape[2]
    wide = 2 * kv + 2 * rope.shape[2]
    return pl.pallas_call(
        query_kernel,
        out_shape=jax.ShapeDtypeStruct((copies, requests, wide), BF16),
        in_specs=[anywhere(), anywhere(), anywhere()],
        out_specs=anywhere(),
        scratch_shapes=[
            pltpu.VMEM(nope.shape, BF16),
            pltpu.VMEM(rope.shape, BF16),
            pltpu.VMEM((2, width, kv), BF16),
            pltpu.VMEM((requests, wide), BF16),
            pltpu.SemaphoreType.DMA((3,)),
            pltpu.SemaphoreType.DMA((copies,)),
        ],
        compiler_params=params(ALL_VMEM),
        name="queries",
    )(nope, rope, key_up)


def gather(lengths, table, own, other):
    width, tokens = own.shape
    return pl.pallas_call(
        gather_kernel,
        out_shape=(
            jax.ShapeDtypeStruct((PLAN,), jnp.int32),
            jax.ShapeDtypeStruct((width, STEPS * CHUNK), BF16),
        ),
        in_specs=[smem(), anywhere(), anywhere(), anywhere()],
        out_specs=(smem(), anywhere()),
        scratch_shapes=[
            pltpu.VMEM(table.shape, jnp.int32),
            pltpu.VMEM((2, width, tokens), BF16),
            pltpu.VMEM((width, STEPS * CHUNK), BF16),
            pltpu.VMEM((16, LANES), jnp.int32),
            pltpu.SMEM((16, LANES), jnp.int32),
            pltpu.SMEM((16,), jnp.int32),
            pltpu.SMEM((16,), jnp.int32),
            pltpu.SemaphoreType.DMA,
            pltpu.SemaphoreType.DMA((2,)),
            pltpu.SemaphoreType.DMA((STEPS,)),
        ],
        compiler_params=params(ALL_VMEM),
        cost_estimate=pl.CostEstimate(
            flops=10_000_000, bytes_accessed=20_000_000, transcendentals=0
        ),
        name="gather",
    )(lengths, table, own, other)


def attend(scale, plan, queries, keys):
    sources, requests, wide = queries.shape
    width = keys.shape[0]
    kv = (wide - 128) // 2
    heads = 2 * sources
    return pl.pallas_call(
        functools.partial(attention_kernel, scale),
        out_shape=jax.ShapeDtypeStruct((sources, requests, wide), BF16),
        in_specs=[smem(), anywhere(), anywhere()],
        out_specs=vmem(),
        scratch_shapes=[
            pltpu.VMEM(queries.shape, BF16),
            pltpu.SemaphoreType.DMA,
            pltpu.VMEM((wide // LANES, sources * requests, LANES), F32),
            pltpu.VMEM((requests, heads, width), BF16),
            pltpu.VMEM((GROUPS, heads, 2 * LANES), F32),
            pltpu.VMEM((requests, heads, LANES), F32),
            pltpu.VMEM((requests, heads, LANES), F32),
            pltpu.VMEM((requests, heads, kv), F32),
            pltpu.VMEM(keys.shape, BF16),
            pltpu.SemaphoreType.DMA((STEPS,)),
        ],
        compiler_params=params(40 * MIB),
        cost_estimate=pl.CostEstimate(
            flops=1_200_000_000, bytes_accessed=12_000_000, transcendentals=524_288
        ),
        name="attention",
    )(plan, queries, keys)


def fold(parts, value_up, copies):
    sources, requests, wide = parts.shape
    kv, out = value_up.shape[1:]
    return pl.pallas_call(
        fold_kernel,
        out_shape=jax.ShapeDtypeStruct((copies, requests, 3 * LANES), BF16),
        in_specs=[vmem(), anywhere()],
        out_specs=vmem(),
        scratch_shapes=[pltpu.VMEM((2, kv, out), BF16), pltpu.SemaphoreType.DMA],
        compiler_params=params(),
        name="fold",
    )(parts, value_up)


def merge(parts):
    requests = parts.shape[1]
    return pl.pallas_call(
        merge_kernel,
        out_shape=jax.ShapeDtypeStruct((requests, 4 * LANES), BF16),
        in_specs=[vmem()],
        out_specs=vmem(),
        compiler_params=params(),
        name="merge",
    )(parts)


def local(query_nope, query_rope, key_up, value_up, cache, lengths, table):
    scale = float(query_nope.shape[2] + query_rope.shape[2]) ** -0.5
    rows, cols = lax.axis_size("row"), lax.axis_size("col")
    own = cache.T
    other = lax.ppermute(own, "col", [(i, i ^ 1) for i in range(cols)])
    queries = make_queries(query_nope, query_rope, key_up, rows)
    queries = lax.all_to_all(queries, "row", split_axis=0, concat_axis=0, tiled=True)
    plan, keys = gather(lengths, table, own, other)
    parts = attend(scale, plan, queries, keys)
    parts = lax.all_to_all(parts, "row", split_axis=0, concat_axis=0, tiled=True)
    parts = fold(parts, value_up, cols)
    parts = lax.all_to_all(parts, "col", split_axis=0, concat_axis=0, tiled=True)
    return merge(parts)


def solution(mesh):
    placed = (
        P(None, "row", None),
        P(None, "row", None),
        P("row", None, None),
        P("row", None, None),
        P(("row", "col"), None),
        P(),
        P(),
    )
    return jax.shard_map(
        local, mesh=mesh, in_specs=placed, out_specs=P(None, "row"), check_vma=False
    )
```

time: 99.8 us -> 97 us (0.972)
  waiting for transfers between devices: 5.81 us -> 0.01 us
  local copies, waits for them, and re-layouts: 6.34 us -> 10.7 us
  Pallas kernels: 27.6 us -> 23.7 us
  blocking collectives: 43.1 us -> 45.7 us
    pallas_call x1, Pallas kernels: 17 us -> 7.99 us  [attend(): pl.pallas_call(functools.partial(attention_kernel, scale), out_shape=jax....]
    all_to_all x1, waiting for transfers between devices: 5.8 us -> 0.01 us  [local(): lax.all_to_all(queries, 'row', split_axis=0, concat_axis=0, tiled=True)]
    pallas_call x3, Pallas kernels: 9.79 us -> 14.9 us  [the longest x1 13 us: gather(): pl.pallas_call(gather_kernel, out_shape=(jax.ShapeDtypeStruct((PLAN,), jn...]
    all_to_all x1, blocking collectives: 21.3 us -> 25.7 us  [local(): lax.all_to_all(parts, 'row', split_axis=0, concat_axis=0, tiled=True)]
    unnamed x12 -> x16, local copies, waits for them, and re-layouts: 6.34 us -> 10.7 us
    all_to_all x1, blocking collectives: 21.8 us -> 20 us  [local(): lax.all_to_all(parts, 'col', split_axis=0, concat_axis=0, tiled=True)]
  transfers between devices with their start and end apart: 2 -> 2, of which waited for: 1 -> 0; matrix products, arithmetic and copies ran while one was open for 1% -> 0% of each run, Pallas kernels for 9% -> 15%
where the time goes in v2:
time: 97 us; the launch traced here: 96.5 us
  blocking collectives  45.7 us (47%)
  Pallas kernels  23.7 us (24%)
  starting transfers between devices  16.3 us (17%)
  local copies, waits for them, and re-layouts  10.7 us (11%)
    all_to_all x1, blocking collectives, local(): lax.all_to_all(parts, 'row', split_axis=0, concat_axis=0, tiled=True)  25.7 us
    all_to_all x1, blocking collectives, local(): lax.all_to_all(parts, 'col', split_axis=0, concat_axis=0, tiled=True)  20 us
    pallas_call x1, Pallas kernels, gather(): pl.pallas_call(gather_kernel, out_shape=(jax.ShapeDtypeStruct((PLAN,), jn...  13 us
    unnamed x16, local copies, waits for them, and re-layouts  10.7 us
    ppermute x1, starting transfers between devices, local(): other = lax.ppermute(own, 'col', [(i, i ^ 1) for i in range(cols)])  8.78 us
    pallas_call x1, Pallas kernels, attend(): pl.pallas_call(functools.partial(attention_kernel, scale), out_shape=jax....  7.99 us
    all_to_all x1, starting transfers between devices, local(): lax.all_to_all(queries, 'row', split_axis=0, concat_axis=0, tiled=True)  7.52 us
  transfers between devices with their start and end apart: 2, of which 0 were waited for; matrix products, arithmetic and copies ran while one was open for 0% of the time, Pallas kernels for 15%

profile of v2, /device:TPU:1, one launch (start us, length us, event | category | flops | bytes accessed | tf_op | source)
XLA Modules:
  0.0 96.5 jit_solution(7004252695739301174)
XLA Ops:
  0.0 8.8 %collective-permute-start = (bf16[576,4096]{1,0:T(8,128)(2,1)}, bf16[576,4096]{1,0:T(8,128)(2,1)}, u32[]{:S(2)}, u32[]{:S(2)}) collective-permute-start(bf16[576,4096]{1,0:T(8,128)(2,1)} %bitcast.1), channel_id=1, source_target_pairs={{0,1},{1,0},{2,3},{3,2},{4,5},{5,4},{6,7},{7,6},{8,9},{9,8},{10,11... | collective-permute-start | bytes 14155784 | tf_op jit(solution)/shard_map/ppermute | solution.py:494
  8.8 0.0 copy-start.3
  8.8 1.0 %copy-done.3 = bf16[4,128,512]{2,1,0:T(8,128)(2,1)S(1)} copy-done((bf16[4,128,512]{2,1,0:T(8,128)(2,1)S(1)}, bf16[4,128,512]{2,1,0:T(8,128)(2,1)}, u32[]{:S(2)}) %copy-start.3) | copy-done | bytes 524312
  9.8 0.0 copy-start.5
  9.8 0.7 copy-done.5
  10.5 0.0 copy-start.6
  10.5 0.7 copy-done.6
  11.2 1.4 %queries.1 = bf16[32,8,1152]{2,1,0:T(8,128)(2,1)} custom-call(bf16[8,4,128]{2,1,0:T(4,128)(2,1)S(1)} %copy-done.5, bf16[8,4,64]{2,1,0:T(4,128)(2,1)S(1)} %copy-done.6, bf16[4,128,512]{2,1,0:T(8,128)(2,1)S(1)} %copy-done.3), custom_call_target="tpu_custom_call" | custom-call | tf_op jit(solution)/shard_map/queries/pallas_call | solution.py:386
  12.6 7.5 %all-to-all-start = ((bf16[32,8,1152]{2,1,0:T(8,128)(2,1)}), bf16[32,8,1152]{2,1,0:T(8,128)(2,1)S(1)}, u32[]{:S(2)}, u32[]{:S(2)}) async-start(bf16[32,8,1152]{2,1,0:T(8,128)(2,1)} %queries.1), calls=%async_computation | async-start | bytes 1179648 | tf_op jit(solution)/shard_map/all_to_all | solution.py:496
  20.1 0.0 collective-permute-done.other_ref
  20.1 0.0 copy-start.1
  20.1 2.3 %copy-done.1 = bf16[4096,576]{0,1:T(8,128)(2,1)S(1)} copy-done((bf16[4096,576]{0,1:T(8,128)(2,1)S(1)}, bf16[4096,576]{0,1:T(8,128)(2,1)}, u32[]{:S(2)}) %copy-start.1) | copy-done | bytes 4718616
  22.5 0.0 copy-start.4
  22.5 0.9 copy-done.4
  23.4 0.0 copy-start.7
  23.4 0.7 copy-done.7
  24.0 13.0 %gather.1 = (s32[256]{0:T(256)S(1)}, bf16[576,10240]{1,0:T(8,128)(2,1)}) custom-call(s32[8]{0:T(128)S(1)} %copy-done.7, s32[8,4096]{1,0:T(8,128)S(1)} %copy-done.4, bf16[576,4096]{1,0:T(8,128)(2,1)S(1)} %bitcast.2, bf16[576,4096]{1,0:T(8,128)(2,1)} %collective-permute-done.other_ref), custom_call_target="tpu_custom_call" | custom-call | flops 10000000 | bytes 20000000 | tf_op jit(solution)/shard_map/gather/pallas_call | solution.py:406
  37.1 0.0 all-to-all-done.query_any
  37.1 0.0 copy-start
  37.1 4.3 %copy-done = bf16[576,10240]{1,0:T(8,128)(2,1)S(1)} copy-done((bf16[576,10240]{1,0:T(8,128)(2,1)S(1)}, bf16[576,10240]{1,0:T(8,128)(2,1)}, u32[]{:S(2)}) %copy-start) | copy-done | bytes 11796504
  41.4 0.0 copy-start.2
  41.4 8.0 %attention.1 = bf16[32,8,1152]{2,1,0:T(8,128)(2,1)S(1)} custom-call(s32[256]{0:T(256)S(1)} %get-tuple-element.7.plan_ref, bf16[32,8,1152]{2,1,0:T(8,128)(2,1)S(1)} %all-to-all-done.query_any, bf16[576,10240]{1,0:T(8,128)(2,1)S(1)} %copy-done), custom_call_target="tpu_custom_call" | custom-call | flops 1200000000 | bytes 12000000 | tf_op jit(solution)/shard_map/attention/pallas_call | solution.py:439
  49.4 25.7 %all_to_all.15.part_ref = bf16[32,8,1152]{2,1,0:T(8,128)(2,1)S(1)} all-to-all(bf16[32,8,1152]{2,1,0:T(8,128)(2,1)S(1)} %attention.1), channel_id=1, replica_groups=mesh['row'=32,'col'=16] {'row'}, dimensions={0} | all-to-all | bytes 1179648 | tf_op jit(solution)/shard_map/all_to_all | solution.py:499
  75.2 0.0 copy-done.2
  75.2 0.5 fold.1
  75.7 20.0 %all_to_all.16.part_ref = bf16[16,8,384]{2,1,0:T(8,128)(2,1)S(1)} all-to-all(bf16[16,8,384]{2,1,0:T(8,128)(2,1)S(1)} %fold.1), channel_id=1, replica_groups=mesh['row'=32,'col'=16] {'col'}, dimensions={0} | all-to-all | bytes 196608 | tf_op jit(solution)/shard_map/all_to_all | solution.py:501
  95.7 0.8 merge.1
Async XLA Ops:
  0.0 20.1 %collective-permute-start = (bf16[576,4096]{1,0:T(8,128)(2,1)}, bf16[576,4096]{1,0:T(8,128)(2,1)}, u32[]{:S(2)}, u32[]{:S(2)}) collective-permute-start(bf16[576,4096]{1,0:T(8,128)(2,1)} %bitcast.1), channel_id=1, source_target_pairs={{0,1},{1,0},{2,3},{3,2},{4,5},{5,4},{6,7},{7,6},{8,9},{9,8},{10,11... | collective-permute-start | bytes 14155784 | tf_op jit(solution)/shard_map/ppermute | solution.py:494
  8.8 1.0 %copy-start.3 = (bf16[4,128,512]{2,1,0:T(8,128)(2,1)S(1)}, bf16[4,128,512]{2,1,0:T(8,128)(2,1)}, u32[]{:S(2)}) copy-start(bf16[4,128,512]{2,1,0:T(8,128)(2,1)} %up_ref.1) | copy-start | bytes 1572868
  9.8 0.7 copy-start.5
  10.5 0.7 copy-start.6
  12.6 24.5 %all-to-all-start = ((bf16[32,8,1152]{2,1,0:T(8,128)(2,1)}), bf16[32,8,1152]{2,1,0:T(8,128)(2,1)S(1)}, u32[]{:S(2)}, u32[]{:S(2)}) async-start(bf16[32,8,1152]{2,1,0:T(8,128)(2,1)} %queries.1), calls=%async_computation | async-start | bytes 1179648 | tf_op jit(solution)/shard_map/all_to_all | solution.py:496
  20.1 2.3 %copy-start.1 = (bf16[4096,576]{0,1:T(8,128)(2,1)S(1)}, bf16[4096,576]{0,1:T(8,128)(2,1)}, u32[]{:S(2)}) copy-start(bf16[4096,576]{0,1:T(8,128)(2,1)} %param.11) | copy-start | bytes 14155780
  22.5 0.9 copy-start.4
  23.4 0.7 copy-start.7
  37.1 4.4 %copy-start = (bf16[576,10240]{1,0:T(8,128)(2,1)S(1)}, bf16[576,10240]{1,0:T(8,128)(2,1)}, u32[]{:S(2)}) copy-start(bf16[576,10240]{1,0:T(8,128)(2,1)} %get-tuple-element.8.keys_any) | copy-start | bytes 35389444
  41.4 33.7 %copy-start.2 = (bf16[4,512,128]{2,1,0:T(8,128)(2,1)S(1)}, bf16[4,512,128]{2,1,0:T(8,128)(2,1)}, u32[]{:S(2)}) copy-start(bf16[4,512,128]{2,1,0:T(8,128)(2,1)} %up_any.1) | copy-start | bytes 1572868

commit v3 on v2

--- a/solution.py
+++ b/solution.py
@@ -15,7 +15,7 @@
 STEPS = GROUPS // UNROLL
 CHUNK = UNROLL * 2 * LANES
 MIB = 1024 * 1024
-ALL_VMEM = 40 * MIB
+ALL_VMEM = 60 * MIB
 ENTRIES = 64
 TRASH = 180
 PLAN = 256
@@ -453,7 +453,7 @@
             pltpu.VMEM(keys.shape, BF16),
             pltpu.SemaphoreType.DMA((STEPS,)),
         ],
-        compiler_params=params(40 * MIB),
+        compiler_params=params(58 * MIB),
         cost_estimate=pl.CostEstimate(
             flops=1_200_000_000, bytes_accessed=12_000_000, transcendentals=524_288
         ),

time: 97 us -> 88.5 us (0.912)
  local copies, waits for them, and re-layouts: 10.7 us -> 0.82 us
  blocking collectives: 45.7 us -> 43.4 us
  waiting for transfers between devices: 0.01 us -> 2.23 us
  Pallas kernels: 23.7 us -> 25.3 us
    unnamed x16 -> x4, local copies, waits for them, and re-layouts: 10.7 us -> 0.82 us
    all_to_all x1, waiting for transfers between devices: 0.01 us -> 2.23 us  [local(): lax.all_to_all(queries, 'row', split_axis=0, concat_axis=0, tiled=True)]
    all_to_all x1, blocking collectives: 25.7 us -> 24.1 us  [local(): lax.all_to_all(parts, 'row', split_axis=0, concat_axis=0, tiled=True)]
  transfers between devices with their start and end apart: 2 -> 2, of which waited for: 0 -> 1; matrix products, arithmetic and copies ran while one was open for 0% -> 0% of each run, Pallas kernels for 15% -> 18%
where the time goes in v3:
time: 88.5 us; the launch traced here: 88.2 us
  blocking collectives  43.4 us (49%)
  Pallas kernels  25.3 us (29%)
  starting transfers between devices  16.3 us (18%)
  waiting for transfers between devices  2.23 us (3%)
    all_to_all x1, blocking collectives, local(): lax.all_to_all(parts, 'row', split_axis=0, concat_axis=0, tiled=True)  24.1 us
    all_to_all x1, blocking collectives, local(): lax.all_to_all(parts, 'col', split_axis=0, concat_axis=0, tiled=True)  19.3 us
    pallas_call x1, Pallas kernels, gather(): pl.pallas_call(gather_kernel, out_shape=(jax.ShapeDtypeStruct((PLAN,), jn...  13.6 us
    ppermute x1, starting transfers between devices, local(): other = lax.ppermute(own, 'col', [(i, i ^ 1) for i in range(cols)])  8.78 us
    pallas_call x1, Pallas kernels, attend(): pl.pallas_call(functools.partial(attention_kernel, scale), out_shape=jax....  8.14 us
    all_to_all x1, starting transfers between devices, local(): lax.all_to_all(queries, 'row', split_axis=0, concat_axis=0, tiled=True)  7.52 us
    pallas_call x1, Pallas kernels, make_queries(): pl.pallas_call(query_kernel, out_shape=jax.ShapeDtypeStruct((copies, requ...  2.26 us
    all_to_all x1, waiting for transfers between devices, local(): lax.all_to_all(queries, 'row', split_axis=0, concat_axis=0, tiled=True)  2.23 us
  transfers between devices with their start and end apart: 2, of which 1 were waited for; matrix products, arithmetic and copies ran while one was open for 0% of the time, Pallas kernels for 18%

profile of v3, /device:TPU:1, one launch (start us, length us, event | category | flops | bytes accessed | tf_op | source)
XLA Modules:
  0.0 88.2 jit_solution(7860900854769958007)
XLA Ops:
  0.0 8.8 %collective-permute-start = (bf16[576,4096]{1,0:T(8,128)(2,1)}, bf16[576,4096]{1,0:T(8,128)(2,1)}, u32[]{:S(2)}, u32[]{:S(2)}) collective-permute-start(bf16[576,4096]{1,0:T(8,128)(2,1)} %bitcast.1), channel_id=1, source_target_pairs={{0,1},{1,0},{2,3},{3,2},{4,5},{5,4},{6,7},{7,6},{8,9},{9,8},{10,11... | collective-permute-start | bytes 14155784 | tf_op jit(solution)/shard_map/ppermute | solution.py:494
  8.8 2.3 %queries.1 = bf16[32,8,1152]{2,1,0:T(8,128)(2,1)} custom-call(bf16[8,4,128]{2,1,0:T(4,128)(2,1)} %nope_any.1, bf16[8,4,64]{2,1,0:T(4,128)(2,1)} %rope_any.1, bf16[4,128,512]{2,1,0:T(8,128)(2,1)} %up_ref.1), custom_call_target="tpu_custom_call" | custom-call | tf_op jit(solution)/shard_map/queries/pallas_call | solution.py:386
  11.1 7.5 %all-to-all-start = ((bf16[32,8,1152]{2,1,0:T(8,128)(2,1)}), bf16[32,8,1152]{2,1,0:T(8,128)(2,1)S(1)}, u32[]{:S(2)}, u32[]{:S(2)}) async-start(bf16[32,8,1152]{2,1,0:T(8,128)(2,1)} %queries.1), calls=%async_computation | async-start | bytes 1179648 | tf_op jit(solution)/shard_map/all_to_all | solution.py:496
  18.6 0.0 collective-permute-done.other_ref
  18.6 13.6 %gather.1 = (s32[256]{0:T(256)}, bf16[576,10240]{1,0:T(8,128)(2,1)}) custom-call(s32[8]{0:T(128)} %length_ref.1, s32[8,4096]{1,0:T(8,128)} %table_any.1, bf16[576,4096]{1,0:T(8,128)(2,1)} %bitcast.2, bf16[576,4096]{1,0:T(8,128)(2,1)} %collective-permute-done.other_ref), custom_call_target="tpu_custom_call" | custom-call | flops 10000000 | bytes 20000000 | tf_op jit(solution)/shard_map/gather/pallas_call | solution.py:406
  32.2 2.2 %all-to-all-done.query_any = bf16[32,8,1152]{2,1,0:T(8,128)(2,1)S(1)} async-done(((bf16[32,8,1152]{2,1,0:T(8,128)(2,1)}), bf16[32,8,1152]{2,1,0:T(8,128)(2,1)S(1)}, u32[]{:S(2)}, u32[]{:S(2)}) %all-to-all-start) | async-done | bytes 589856 | tf_op jit(solution)/shard_map/all_to_all | solution.py:496
  34.4 0.0 copy-start.1
  34.4 0.8 copy-done.1
  35.3 0.0 copy-start
  35.3 8.1 %attention.1 = bf16[32,8,1152]{2,1,0:T(8,128)(2,1)} custom-call(s32[256]{0:T(256)} %get-tuple-element.7.plan_ref, bf16[32,8,1152]{2,1,0:T(8,128)(2,1)} %copy-done.1, bf16[576,10240]{1,0:T(8,128)(2,1)} %get-tuple-element.8.keys_any), custom_call_target="tpu_custom_call" | custom-call | flops 1200000000 | bytes 12000000 | tf_op jit(solution)/shard_map/attention/pallas_call | solution.py:439
  43.4 24.1 %all_to_all.15.part_ref = bf16[32,8,1152]{2,1,0:T(8,128)(2,1)S(1)} all-to-all(bf16[32,8,1152]{2,1,0:T(8,128)(2,1)} %attention.1), channel_id=1, replica_groups=mesh['row'=32,'col'=16] {'row'}, dimensions={0} | all-to-all | bytes 1179648 | tf_op jit(solution)/shard_map/all_to_all | solution.py:499
  67.5 0.0 copy-done
  67.5 0.5 fold.1
  68.0 19.3 %all_to_all.16.part_ref = bf16[16,8,384]{2,1,0:T(8,128)(2,1)S(1)} all-to-all(bf16[16,8,384]{2,1,0:T(8,128)(2,1)S(1)} %fold.1), channel_id=1, replica_groups=mesh['row'=32,'col'=16] {'col'}, dimensions={0} | all-to-all | bytes 196608 | tf_op jit(solution)/shard_map/all_to_all | solution.py:501
  87.3 0.8 merge.1
Async XLA Ops:
  0.0 18.6 %collective-permute-start = (bf16[576,4096]{1,0:T(8,128)(2,1)}, bf16[576,4096]{1,0:T(8,128)(2,1)}, u32[]{:S(2)}, u32[]{:S(2)}) collective-permute-start(bf16[576,4096]{1,0:T(8,128)(2,1)} %bitcast.1), channel_id=1, source_target_pairs={{0,1},{1,0},{2,3},{3,2},{4,5},{5,4},{6,7},{7,6},{8,9},{9,8},{10,11... | collective-permute-start | bytes 14155784 | tf_op jit(solution)/shard_map/ppermute | solution.py:494
  11.1 23.4 %all-to-all-start = ((bf16[32,8,1152]{2,1,0:T(8,128)(2,1)}), bf16[32,8,1152]{2,1,0:T(8,128)(2,1)S(1)}, u32[]{:S(2)}, u32[]{:S(2)}) async-start(bf16[32,8,1152]{2,1,0:T(8,128)(2,1)} %queries.1), calls=%async_computation | async-start | bytes 1179648 | tf_op jit(solution)/shard_map/all_to_all | solution.py:496
  34.4 0.8 copy-start.1
  35.3 32.2 %copy-start = (bf16[4,512,128]{2,1,0:T(8,128)(2,1)S(1)}, bf16[4,512,128]{2,1,0:T(8,128)(2,1)}, u32[]{:S(2)}) copy-start(bf16[4,512,128]{2,1,0:T(8,128)(2,1)} %up_any.1) | copy-start | bytes 1572868

commit v4 on v3

--- a/solution.py
+++ b/solution.py
@@ -18,7 +18,8 @@
 ALL_VMEM = 60 * MIB
 ENTRIES = 64
 TRASH = 180
-PLAN = 256
+PLAN = 1024
+SPREAD = 6 * 1024 * 1024
 F32 = jnp.float32
 BF16 = jnp.bfloat16
 
@@ -84,8 +85,9 @@
     table_any,
     own_ref,
     other_ref,
+    plan_any,
+    keys_ref,
     plan_ref,
-    keys_ref,
     table_ref,
     cache,
     keys,
@@ -94,6 +96,7 @@
     count,
     fill,
     sem,
+    plan_sem,
     cache_sems,
     out_sems,
 ):
@@ -173,6 +176,8 @@
         fill[owner] = at + jnp.where(owner > 0, 1, 0)
         plan_ref[ENTRIES + at] = t + (rows << 8)
 
+    plan_store = pltpu.make_async_copy(plan_ref, plan_any.at[pl.ds(0, PLAN)], plan_sem)
+    plan_store.start()
     for load in loads:
         load.wait()
     steps = (plan_ref[0] + UNROLL - 1) // UNROLL
@@ -187,33 +192,33 @@
         return jnp.concatenate([tile[:, PAGE:], tile[:, :PAGE]], axis=1)
 
     def chunk(step):
-        at = pl.ds(pl.multiple_of(step * CHUNK, CHUNK), CHUNK)
-        return pltpu.make_async_copy(keys.at[:, at], keys_ref.at[:, at], out_sems.at[step])
+        return pltpu.make_async_copy(keys.at[step], keys_ref.at[step], out_sems.at[step])
 
     @pl.loop(0, steps)
     def _(step):
-        @pl.loop(step * 2 * UNROLL, (step + 1) * 2 * UNROLL)
+        @pl.loop(0, 2 * UNROLL)
         def _(j):
-            first = plan_ref[ENTRIES + 2 * j]
-            second = plan_ref[ENTRIES + 2 * j + 1]
+            entry = ENTRIES + 2 * (2 * UNROLL * step + j)
+            first = plan_ref[entry]
+            second = plan_ref[entry + 1]
             kind = (first & 1) + 2 * (second & 1)
             at = pl.ds(pl.multiple_of(j * LANES, LANES), LANES)
 
             @pl.when(kind == 2)
             def _():
-                keys[:, at] = jnp.where(left_half, tile_of(first), tile_of(second))
+                keys[step, :, at] = jnp.where(left_half, tile_of(first), tile_of(second))
 
             @pl.when(kind == 0)
             def _():
-                keys[:, at] = jnp.where(left_half, tile_of(first), turned(tile_of(second)))
+                keys[step, :, at] = jnp.where(left_half, tile_of(first), turned(tile_of(second)))
 
             @pl.when(kind == 3)
             def _():
-                keys[:, at] = jnp.where(left_half, turned(tile_of(first)), tile_of(second))
+                keys[step, :, at] = jnp.where(left_half, turned(tile_of(first)), tile_of(second))
 
             @pl.when(kind == 1)
             def _():
-                keys[:, at] = turned(jnp.where(left_half, tile_of(second), tile_of(first)))
+                keys[step, :, at] = turned(jnp.where(left_half, tile_of(second), tile_of(first)))
 
         chunk(step).start()
 
@@ -221,18 +226,22 @@
     def _(step):
         chunk(step).wait()
 
+    plan_store.wait()
+
 
 def attention_kernel(
-    scale, plan_ref, query_any, keys_any, out_ref, query_ref, query_sem, staged, query, scores, top, denom, total, keys_ref, sems
+    scale, plan_any, query_any, keys_any, out_ref, plan_ref, plan_sem, query_ref, query_sem, staged, query, scores, top, denom, total, keys_ref, sems
 ):
     load = pltpu.make_async_copy(query_any, query_ref, query_sem)
     load.start()
+    fetch = pltpu.make_async_copy(plan_any.at[pl.ds(0, PLAN)], plan_ref, plan_sem)
+    fetch.start()
+    fetch.wait()
     groups = plan_ref[0]
     steps = (groups + UNROLL - 1) // UNROLL
 
     def chunk(step):
-        at = pl.ds(pl.multiple_of(step * CHUNK, CHUNK), CHUNK)
-        return pltpu.make_async_copy(keys_any.at[:, at], keys_ref.at[:, at], sems.at[step])
+        return pltpu.make_async_copy(keys_any.at[step], keys_ref.at[step], sems.at[step])
 
     @pl.loop(0, steps)
     def _(step):
@@ -261,8 +270,8 @@
     left_half = lane < PAGE
     within = lane & (PAGE - 1)
 
-    def keys(g, depth):
-        return keys_ref[:depth, pl.ds(pl.multiple_of(g * 2 * LANES, 2 * LANES), 2 * LANES)]
+    def keys(step, u, depth):
+        return keys_ref[step, :depth, 2 * LANES * u : 2 * LANES * (u + 1)]
 
     @pl.loop(0, steps)
     def _(step):
@@ -270,7 +279,7 @@
         for u in range(UNROLL):
             g = step * UNROLL + u
             r = plan_ref[8 + g]
-            score = jnp.dot(query[r], keys(g, keys_ref.shape[0]), preferred_element_type=F32)
+            score = jnp.dot(query[r], keys(step, u, keys_ref.shape[1]), preferred_element_type=F32)
             halves = []
             for half in range(2):
                 rows = jnp.where(
@@ -301,7 +310,7 @@
             denom[r] = denom[r] + halves[0].astype(F32) + halves[1].astype(F32)
             total[r] = total[r] + lax.dot_general(
                 jnp.concatenate(halves, axis=1),
-                keys(g, kv),
+                keys(step, u, kv),
                 (((1,), (1,)), ((), ())),
                 preferred_element_type=F32,
             )
@@ -406,19 +415,21 @@
     return pl.pallas_call(
         gather_kernel,
         out_shape=(
-            jax.ShapeDtypeStruct((PLAN,), jnp.int32),
-            jax.ShapeDtypeStruct((width, STEPS * CHUNK), BF16),
+            jax.ShapeDtypeStruct((SPREAD,), jnp.int32),
+            jax.ShapeDtypeStruct((2 * STEPS, width, CHUNK), BF16),
         ),
         in_specs=[smem(), anywhere(), anywhere(), anywhere()],
-        out_specs=(smem(), anywhere()),
+        out_specs=(anywhere(), anywhere()),
         scratch_shapes=[
+            pltpu.SMEM((PLAN,), jnp.int32),
             pltpu.VMEM(table.shape, jnp.int32),
             pltpu.VMEM((2, width, tokens), BF16),
-            pltpu.VMEM((width, STEPS * CHUNK), BF16),
+            pltpu.VMEM((STEPS, width, CHUNK), BF16),
             pltpu.VMEM((16, LANES), jnp.int32),
             pltpu.SMEM((16, LANES), jnp.int32),
             pltpu.SMEM((16,), jnp.int32),
             pltpu.SMEM((16,), jnp.int32),
+            pltpu.SemaphoreType.DMA,
             pltpu.SemaphoreType.DMA,
             pltpu.SemaphoreType.DMA((2,)),
             pltpu.SemaphoreType.DMA((STEPS,)),
@@ -433,15 +444,17 @@
 
 def attend(scale, plan, queries, keys):
     sources, requests, wide = queries.shape
-    width = keys.shape[0]
+    width = keys.shape[1]
     kv = (wide - 128) // 2
     heads = 2 * sources
     return pl.pallas_call(
         functools.partial(attention_kernel, scale),
         out_shape=jax.ShapeDtypeStruct((sources, requests, wide), BF16),
-        in_specs=[smem(), anywhere(), anywhere()],
+        in_specs=[anywhere(), anywhere(), anywhere()],
         out_specs=vmem(),
         scratch_shapes=[
+            pltpu.SMEM((PLAN,), jnp.int32),
+            pltpu.SemaphoreType.DMA,
             pltpu.VMEM(queries.shape, BF16),
             pltpu.SemaphoreType.DMA,
             pltpu.VMEM((wide // LANES, sources * requests, LANES), F32),
@@ -450,10 +463,10 @@
             pltpu.VMEM((requests, heads, LANES), F32),
             pltpu.VMEM((requests, heads, LANES), F32),
             pltpu.VMEM((requests, heads, kv), F32),
-            pltpu.VMEM(keys.shape, BF16),
+            pltpu.VMEM((STEPS, width, CHUNK), BF16),
             pltpu.SemaphoreType.DMA((STEPS,)),
         ],
-        compiler_params=params(58 * MIB),
+        compiler_params=params(40 * MIB),
         cost_estimate=pl.CostEstimate(
             flops=1_200_000_000, bytes_accessed=12_000_000, transcendentals=524_288
         ),

time: 88.5 us -> 85.7 us (0.968)
  blocking collectives: 43.4 us -> 41.7 us
    all_to_all x1, blocking collectives: 19.3 us -> 18.4 us  [local(): lax.all_to_all(parts, 'col', split_axis=0, concat_axis=0, tiled=True)]
  transfers between devices with their start and end apart: 2 -> 2, of which waited for: 1 -> 1; matrix products, arithmetic and copies ran while one was open for 0% -> 0% of each run, Pallas kernels for 18% -> 19%
where the time goes in v4:
time: 85.7 us; the launch traced here: 85.4 us
  blocking collectives  41.7 us (49%)
  Pallas kernels  25.6 us (30%)
  starting transfers between devices  16.3 us (19%)
  waiting for transfers between devices  1.75 us (2%)
    all_to_all x1, blocking collectives, local(): lax.all_to_all(parts, 'row', split_axis=0, concat_axis=0, tiled=True)  23.3 us
    all_to_all x1, blocking collectives, local(): lax.all_to_all(parts, 'col', split_axis=0, concat_axis=0, tiled=True)  18.4 us
    pallas_call x1, Pallas kernels, gather(): pl.pallas_call(gather_kernel, out_shape=(jax.ShapeDtypeStruct((SPREAD,),...  14.1 us
    ppermute x1, starting transfers between devices, local(): other = lax.ppermute(own, 'col', [(i, i ^ 1) for i in range(cols)])  8.78 us
    pallas_call x1, Pallas kernels, attend(): pl.pallas_call(functools.partial(attention_kernel, scale), out_shape=jax....  7.95 us
    all_to_all x1, starting transfers between devices, local(): lax.all_to_all(queries, 'row', split_axis=0, concat_axis=0, tiled=True)  7.52 us
    pallas_call x1, Pallas kernels, make_queries(): pl.pallas_call(query_kernel, out_shape=jax.ShapeDtypeStruct((copies, requ...  2.26 us
    all_to_all x1, waiting for transfers between devices, local(): lax.all_to_all(queries, 'row', split_axis=0, concat_axis=0, tiled=True)  1.74 us
  transfers between devices with their start and end apart: 2, of which 1 were waited for; matrix products, arithmetic and copies ran while one was open for 0% of the time, Pallas kernels for 19%

profile of v4, /device:TPU:1, one launch (start us, length us, event | category | flops | bytes accessed | tf_op | source)
XLA Modules:
  0.0 85.4 jit_solution(10109063234806112108)
XLA Ops:
  0.0 8.8 %collective-permute-start = (bf16[576,4096]{1,0:T(8,128)(2,1)}, bf16[576,4096]{1,0:T(8,128)(2,1)}, u32[]{:S(2)}, u32[]{:S(2)}) collective-permute-start(bf16[576,4096]{1,0:T(8,128)(2,1)} %bitcast.1), channel_id=1, source_target_pairs={{0,1},{1,0},{2,3},{3,2},{4,5},{5,4},{6,7},{7,6},{8,9},{9,8},{10,11... | collective-permute-start | bytes 14155784 | tf_op jit(solution)/shard_map/ppermute | solution.py:507
  8.8 2.3 %queries.1 = bf16[32,8,1152]{2,1,0:T(8,128)(2,1)} custom-call(bf16[8,4,128]{2,1,0:T(4,128)(2,1)} %nope_any.1, bf16[8,4,64]{2,1,0:T(4,128)(2,1)} %rope_any.1, bf16[4,128,512]{2,1,0:T(8,128)(2,1)} %up_ref.1), custom_call_target="tpu_custom_call" | custom-call | tf_op jit(solution)/shard_map/queries/pallas_call | solution.py:395
  11.1 7.5 %all-to-all-start = ((bf16[32,8,1152]{2,1,0:T(8,128)(2,1)}), bf16[32,8,1152]{2,1,0:T(8,128)(2,1)S(1)}, u32[]{:S(2)}, u32[]{:S(2)}) async-start(bf16[32,8,1152]{2,1,0:T(8,128)(2,1)} %queries.1), calls=%async_computation | async-start | bytes 1179648 | tf_op jit(solution)/shard_map/all_to_all | solution.py:509
  18.6 0.0 collective-permute-done.other_ref
  18.6 14.1 %gather.1 = (s32[6291456]{0:T(1024)}, bf16[20,576,1024]{2,1,0:T(8,128)(2,1)}) custom-call(s32[8]{0:T(128)} %length_ref.1, s32[8,4096]{1,0:T(8,128)} %table_any.1, bf16[576,4096]{1,0:T(8,128)(2,1)} %bitcast.2, bf16[576,4096]{1,0:T(8,128)(2,1)} %collective-permute-done.other_ref), custom_call_target="tpu_custom_call" | custom-call | flops 10000000 | bytes 20000000 | tf_op jit(solution)/shard_map/gather/pallas_call | solution.py:415
  32.7 1.7 %all-to-all-done.query_any = bf16[32,8,1152]{2,1,0:T(8,128)(2,1)S(1)} async-done(((bf16[32,8,1152]{2,1,0:T(8,128)(2,1)}), bf16[32,8,1152]{2,1,0:T(8,128)(2,1)S(1)}, u32[]{:S(2)}, u32[]{:S(2)}) %all-to-all-start) | async-done | bytes 589856 | tf_op jit(solution)/shard_map/all_to_all | solution.py:509
  34.4 0.0 copy-start
  34.4 7.9 %attention.1 = bf16[32,8,1152]{2,1,0:T(8,128)(2,1)S(1)} custom-call(s32[6291456]{0:T(1024)} %get-tuple-element.7.plan_any, bf16[32,8,1152]{2,1,0:T(8,128)(2,1)S(1)} %all-to-all-done.query_any, bf16[20,576,1024]{2,1,0:T(8,128)(2,1)} %get-tuple-element.8.keys_any), custom_call_target="tpu_custom_call" | custom-call | flops 1200000000 | bytes 12000000 | tf_op jit(solution)/shard_map/attention/pallas_call | solution.py:450
  42.4 23.3 %all_to_all.15.part_ref = bf16[32,8,1152]{2,1,0:T(8,128)(2,1)S(1)} all-to-all(bf16[32,8,1152]{2,1,0:T(8,128)(2,1)S(1)} %attention.1), channel_id=1, replica_groups=mesh['row'=32,'col'=16] {'row'}, dimensions={0} | all-to-all | bytes 1179648 | tf_op jit(solution)/shard_map/all_to_all | solution.py:512
  65.7 0.0 copy-done
  65.7 0.5 fold.1
  66.2 18.4 %all_to_all.16.part_ref = bf16[16,8,384]{2,1,0:T(8,128)(2,1)S(1)} all-to-all(bf16[16,8,384]{2,1,0:T(8,128)(2,1)S(1)} %fold.1), channel_id=1, replica_groups=mesh['row'=32,'col'=16] {'col'}, dimensions={0} | all-to-all | bytes 196608 | tf_op jit(solution)/shard_map/all_to_all | solution.py:514
  84.6 0.8 merge.1
Async XLA Ops:
  0.0 18.6 %collective-permute-start = (bf16[576,4096]{1,0:T(8,128)(2,1)}, bf16[576,4096]{1,0:T(8,128)(2,1)}, u32[]{:S(2)}, u32[]{:S(2)}) collective-permute-start(bf16[576,4096]{1,0:T(8,128)(2,1)} %bitcast.1), channel_id=1, source_target_pairs={{0,1},{1,0},{2,3},{3,2},{4,5},{5,4},{6,7},{7,6},{8,9},{9,8},{10,11... | collective-permute-start | bytes 14155784 | tf_op jit(solution)/shard_map/ppermute | solution.py:507
  11.1 23.4 %all-to-all-start = ((bf16[32,8,1152]{2,1,0:T(8,128)(2,1)}), bf16[32,8,1152]{2,1,0:T(8,128)(2,1)S(1)}, u32[]{:S(2)}, u32[]{:S(2)}) async-start(bf16[32,8,1152]{2,1,0:T(8,128)(2,1)} %queries.1), calls=%async_computation | async-start | bytes 1179648 | tf_op jit(solution)/shard_map/all_to_all | solution.py:509
  34.4 31.3 %copy-start = (bf16[4,512,128]{2,1,0:T(8,128)(2,1)S(1)}, bf16[4,512,128]{2,1,0:T(8,128)(2,1)}, u32[]{:S(2)}) copy-start(bf16[4,512,128]{2,1,0:T(8,128)(2,1)} %up_any.1) | copy-start | bytes 1572868

commit v5 on v4

--- a/solution.py
+++ b/solution.py
@@ -19,6 +19,7 @@
 ENTRIES = 64
 TRASH = 180
 PLAN = 1024
+EARLY = 3
 SPREAD = 6 * 1024 * 1024
 F32 = jnp.float32
 BF16 = jnp.bfloat16
@@ -236,20 +237,23 @@
     load.start()
     fetch = pltpu.make_async_copy(plan_any.at[pl.ds(0, PLAN)], plan_ref, plan_sem)
     fetch.start()
+
+    def chunk(step):
+        return pltpu.make_async_copy(keys_any.at[step], keys_ref.at[step], sems.at[step])
+
+    sources, requests, wide = query_ref.shape
+    kv = total.shape[2]
+    tiles = kv // LANES
+    for step in range(EARLY):
+        chunk(step).start()
     fetch.wait()
     groups = plan_ref[0]
     steps = (groups + UNROLL - 1) // UNROLL
 
-    def chunk(step):
-        return pltpu.make_async_copy(keys_any.at[step], keys_ref.at[step], sems.at[step])
-
-    @pl.loop(0, steps)
+    @pl.loop(EARLY, jnp.maximum(steps, EARLY))
     def _(step):
         chunk(step).start()
 
-    sources, requests, wide = query_ref.shape
-    kv = total.shape[2]
-    tiles = kv // LANES
     top[...] = jnp.full_like(top, EMPTY)
     denom[...] = jnp.zeros_like(denom)
     total[...] = jnp.zeros_like(total)
@@ -292,6 +296,10 @@
                 scores[g, :, half * LANES : (half + 1) * LANES] = part
                 halves.append(part)
             top[r] = jnp.maximum(top[r], jnp.maximum(*halves))
+
+    @pl.loop(jnp.minimum(steps, EARLY), EARLY)
+    def _(step):
+        chunk(step).wait()
 
     for r in range(requests):
         top[r] = jnp.broadcast_to(jnp.max(top[r], axis=1, keepdims=True), top.shape[1:])

time: 85.7 us -> 85.7 us (level)
  no operation moved by 1% of the time
where the time goes in v5:
time: 85.7 us; the launch traced here: 85 us
  blocking collectives  41.9 us (49%)
  Pallas kernels  25.2 us (29%)
  starting transfers between devices  16.3 us (19%)
  waiting for transfers between devices  1.55 us (2%)
    all_to_all x1, blocking collectives, local(): lax.all_to_all(parts, 'row', split_axis=0, concat_axis=0, tiled=True)  22.8 us
    all_to_all x1, blocking collectives, local(): lax.all_to_all(parts, 'col', split_axis=0, concat_axis=0, tiled=True)  19.1 us
    pallas_call x1, Pallas kernels, gather(): pl.pallas_call(gather_kernel, out_shape=(jax.ShapeDtypeStruct((SPREAD,),...  14.3 us
    ppermute x1, starting transfers between devices, local(): other = lax.ppermute(own, 'col', [(i, i ^ 1) for i in range(cols)])  8.78 us
    all_to_all x1, starting transfers between devices, local(): lax.all_to_all(queries, 'row', split_axis=0, concat_axis=0, tiled=True)  7.52 us
    pallas_call x1, Pallas kernels, attend(): pl.pallas_call(functools.partial(attention_kernel, scale), out_shape=jax....  7.33 us
    pallas_call x1, Pallas kernels, make_queries(): pl.pallas_call(query_kernel, out_shape=jax.ShapeDtypeStruct((copies, requ...  2.26 us
  transfers between devices with their start and end apart: 2, of which 1 were waited for; matrix products, arithmetic and copies ran while one was open for 0% of the time, Pallas kernels for 19%

profile of v5, /device:TPU:1, one launch (start us, length us, event | category | flops | bytes accessed | tf_op | source)
XLA Modules:
  0.0 85.0 jit_solution(7184255679994989847)
XLA Ops:
  0.0 8.8 %collective-permute-start = (bf16[576,4096]{1,0:T(8,128)(2,1)}, bf16[576,4096]{1,0:T(8,128)(2,1)}, u32[]{:S(2)}, u32[]{:S(2)}) collective-permute-start(bf16[576,4096]{1,0:T(8,128)(2,1)} %bitcast.1), channel_id=1, source_target_pairs={{0,1},{1,0},{2,3},{3,2},{4,5},{5,4},{6,7},{7,6},{8,9},{9,8},{10,11... | collective-permute-start | bytes 14155784 | tf_op jit(solution)/shard_map/ppermute | solution.py:515
  8.8 2.3 %queries.1 = bf16[32,8,1152]{2,1,0:T(8,128)(2,1)} custom-call(bf16[8,4,128]{2,1,0:T(4,128)(2,1)} %nope_any.1, bf16[8,4,64]{2,1,0:T(4,128)(2,1)} %rope_any.1, bf16[4,128,512]{2,1,0:T(8,128)(2,1)} %up_ref.1), custom_call_target="tpu_custom_call" | custom-call | tf_op jit(solution)/shard_map/queries/pallas_call | solution.py:403
  11.1 7.5 %all-to-all-start = ((bf16[32,8,1152]{2,1,0:T(8,128)(2,1)}), bf16[32,8,1152]{2,1,0:T(8,128)(2,1)S(1)}, u32[]{:S(2)}, u32[]{:S(2)}) async-start(bf16[32,8,1152]{2,1,0:T(8,128)(2,1)} %queries.1), calls=%async_computation | async-start | bytes 1179648 | tf_op jit(solution)/shard_map/all_to_all | solution.py:517
  18.6 0.0 collective-permute-done.other_ref
  18.6 14.3 %gather.1 = (s32[6291456]{0:T(1024)}, bf16[20,576,1024]{2,1,0:T(8,128)(2,1)}) custom-call(s32[8]{0:T(128)} %length_ref.1, s32[8,4096]{1,0:T(8,128)} %table_any.1, bf16[576,4096]{1,0:T(8,128)(2,1)} %bitcast.2, bf16[576,4096]{1,0:T(8,128)(2,1)} %collective-permute-done.other_ref), custom_call_target="tpu_custom_call" | custom-call | flops 10000000 | bytes 20000000 | tf_op jit(solution)/shard_map/gather/pallas_call | solution.py:423
  32.9 1.5 %all-to-all-done.query_any = bf16[32,8,1152]{2,1,0:T(8,128)(2,1)S(1)} async-done(((bf16[32,8,1152]{2,1,0:T(8,128)(2,1)}), bf16[32,8,1152]{2,1,0:T(8,128)(2,1)S(1)}, u32[]{:S(2)}, u32[]{:S(2)}) %all-to-all-start) | async-done | bytes 589856 | tf_op jit(solution)/shard_map/all_to_all | solution.py:517
  34.4 0.0 copy-start
  34.4 7.3 %attention.1 = bf16[32,8,1152]{2,1,0:T(8,128)(2,1)S(1)} custom-call(s32[6291456]{0:T(1024)} %get-tuple-element.7.plan_any, bf16[32,8,1152]{2,1,0:T(8,128)(2,1)S(1)} %all-to-all-done.query_any, bf16[20,576,1024]{2,1,0:T(8,128)(2,1)} %get-tuple-element.8.keys_any), custom_call_target="tpu_custom_call" | custom-call | flops 1200000000 | bytes 12000000 | tf_op jit(solution)/shard_map/attention/pallas_call | solution.py:458
  41.8 22.8 %all_to_all.15.part_ref = bf16[32,8,1152]{2,1,0:T(8,128)(2,1)S(1)} all-to-all(bf16[32,8,1152]{2,1,0:T(8,128)(2,1)S(1)} %attention.1), channel_id=1, replica_groups=mesh['row'=32,'col'=16] {'row'}, dimensions={0} | all-to-all | bytes 1179648 | tf_op jit(solution)/shard_map/all_to_all | solution.py:520
  64.6 0.0 copy-done
  64.6 0.5 fold.1
  65.1 19.1 %all_to_all.16.part_ref = bf16[16,8,384]{2,1,0:T(8,128)(2,1)S(1)} all-to-all(bf16[16,8,384]{2,1,0:T(8,128)(2,1)S(1)} %fold.1), channel_id=1, replica_groups=mesh['row'=32,'col'=16] {'col'}, dimensions={0} | all-to-all | bytes 196608 | tf_op jit(solution)/shard_map/all_to_all | solution.py:522
  84.2 0.8 merge.1
Async XLA Ops:
  0.0 18.6 %collective-permute-start = (bf16[576,4096]{1,0:T(8,128)(2,1)}, bf16[576,4096]{1,0:T(8,128)(2,1)}, u32[]{:S(2)}, u32[]{:S(2)}) collective-permute-start(bf16[576,4096]{1,0:T(8,128)(2,1)} %bitcast.1), channel_id=1, source_target_pairs={{0,1},{1,0},{2,3},{3,2},{4,5},{5,4},{6,7},{7,6},{8,9},{9,8},{10,11... | collective-permute-start | bytes 14155784 | tf_op jit(solution)/shard_map/ppermute | solution.py:515
  11.1 23.4 %all-to-all-start = ((bf16[32,8,1152]{2,1,0:T(8,128)(2,1)}), bf16[32,8,1152]{2,1,0:T(8,128)(2,1)S(1)}, u32[]{:S(2)}, u32[]{:S(2)}) async-start(bf16[32,8,1152]{2,1,0:T(8,128)(2,1)} %queries.1), calls=%async_computation | async-start | bytes 1179648 | tf_op jit(solution)/shard_map/all_to_all | solution.py:517
  34.4 30.1 %copy-start = (bf16[4,512,128]{2,1,0:T(8,128)(2,1)S(1)}, bf16[4,512,128]{2,1,0:T(8,128)(2,1)}, u32[]{:S(2)}) copy-start(bf16[4,512,128]{2,1,0:T(8,128)(2,1)} %up_any.1) | copy-start | bytes 1572868

commit v6 on v5

--- a/solution.py
+++ b/solution.py
@@ -11,14 +11,15 @@
 LANES = 128
 EMPTY = -1e30
 UNROLL = 4
-GROUPS = 40
+GROUPS = 36
 STEPS = GROUPS // UNROLL
 CHUNK = UNROLL * 2 * LANES
 MIB = 1024 * 1024
 ALL_VMEM = 60 * MIB
-ENTRIES = 64
+ENTRIES = 128
 TRASH = 180
 PLAN = 1024
+SPARE = 15
 EARLY = 3
 SPREAD = 6 * 1024 * 1024
 F32 = jnp.float32
@@ -154,21 +155,23 @@
     start = jnp.int32(0)
     fill[0] = TRASH
     for r in range(requests):
-        fill[r + 1] = 4 * start
-        groups = (count[r + 1] + 3) >> 2
-
-        @pl.loop(start, start + groups)
-        def _(g):
-            plan_ref[8 + g] = r
-            for at in range(4):
-                plan_ref[ENTRIES + 4 * g + at] = 0
-
-        start = start + groups
+        fill[r + 1] = 2 * start
+        tiles = (count[r + 1] + 1) >> 1
+
+        @pl.loop(start, start + tiles)
+        def _(t):
+            plan_ref[8 + t] = r
+
+        @pl.when(tiles > 0)
+        def _():
+            plan_ref[ENTRIES + 2 * (start + tiles) - 1] = 0
+
+        start = start + tiles
     plan_ref[0] = start
-    for ahead in range(UNROLL - 1):
+    for ahead in range(2 * UNROLL - 1):
         plan_ref[8 + start + ahead] = 0
-        for at in range(4):
-            plan_ref[ENTRIES + 4 * (start + ahead) + at] = 0
+        for at in range(2):
+            plan_ref[ENTRIES + 2 * (start + ahead) + at] = 0
 
     @pl.loop(0, 128, unroll=8)
     def _(t):
@@ -181,7 +184,7 @@
     plan_store.start()
     for load in loads:
         load.wait()
-    steps = (plan_ref[0] + UNROLL - 1) // UNROLL
+    steps = (plan_ref[0] + 2 * UNROLL - 1) // (2 * UNROLL)
     left_half = lax.broadcasted_iota(jnp.int32, (1, LANES), 1) < PAGE
 
     def tile_of(entry):
@@ -243,12 +246,13 @@
 
     sources, requests, wide = query_ref.shape
     kv = total.shape[2]
+    heads = total.shape[1]
     tiles = kv // LANES
     for step in range(EARLY):
         chunk(step).start()
     fetch.wait()
-    groups = plan_ref[0]
-    steps = (groups + UNROLL - 1) // UNROLL
+    used = plan_ref[0]
+    steps = (used + 2 * UNROLL - 1) // (2 * UNROLL)
 
     @pl.loop(EARLY, jnp.maximum(steps, EARLY))
     def _(step):
@@ -282,20 +286,19 @@
         chunk(step).wait()
         for u in range(UNROLL):
             g = step * UNROLL + u
-            r = plan_ref[8 + g]
-            score = jnp.dot(query[r], keys(step, u, keys_ref.shape[1]), preferred_element_type=F32)
-            halves = []
-            for half in range(2):
+            owners = [plan_ref[8 + 2 * g + half] for half in range(2)]
+            both = jnp.concatenate([query[r] for r in owners], axis=0)
+            score = jnp.dot(both, keys(step, u, keys_ref.shape[1]), preferred_element_type=F32)
+            for half, r in enumerate(owners):
                 rows = jnp.where(
                     left_half,
                     plan_ref[ENTRIES + 4 * g + 2 * half] >> 8,
                     plan_ref[ENTRIES + 4 * g + 2 * half + 1] >> 8,
                 )
-                part = score[:, half * LANES : (half + 1) * LANES]
+                part = score[half * heads : (half + 1) * heads, half * LANES : (half + 1) * LANES]
                 part = jnp.where(within < rows, part, EMPTY)
                 scores[g, :, half * LANES : (half + 1) * LANES] = part
-                halves.append(part)
-            top[r] = jnp.maximum(top[r], jnp.maximum(*halves))
+                top[r] = jnp.maximum(top[r], part)
 
     @pl.loop(jnp.minimum(steps, EARLY), EARLY)
     def _(step):
@@ -308,20 +311,19 @@
     def _(step):
         for u in range(UNROLL):
             g = step * UNROLL + u
-            r = plan_ref[8 + g]
-            level = top[r]
-            live = jnp.where(g < groups, 1.0, 0.0)
-            halves = []
+            values = keys(step, u, kv)
             for half in range(2):
+                r = plan_ref[8 + 2 * g + half]
+                live = jnp.where(2 * g + half < used, 1.0, 0.0)
                 part = scores[g, :, half * LANES : (half + 1) * LANES]
-                halves.append((jnp.exp((part - level) * scale) * live).astype(BF16))
-            denom[r] = denom[r] + halves[0].astype(F32) + halves[1].astype(F32)
-            total[r] = total[r] + lax.dot_general(
-                jnp.concatenate(halves, axis=1),
-                keys(step, u, kv),
-                (((1,), (1,)), ((), ())),
-                preferred_element_type=F32,
-            )
+                expo = (jnp.exp((part - top[r]) * scale) * live).astype(BF16)
+                denom[r] = denom[r] + expo.astype(F32)
+                total[r] = total[r] + lax.dot_general(
+                    expo,
+                    values[:, half * LANES : (half + 1) * LANES],
+                    (((1,), (1,)), ((), ())),
+                    preferred_element_type=F32,
+                )
 
     for r in range(requests):
         sums = jnp.sum(denom[r], axis=1, keepdims=True)
@@ -424,7 +426,7 @@
         gather_kernel,
         out_shape=(
             jax.ShapeDtypeStruct((SPREAD,), jnp.int32),
-            jax.ShapeDtypeStruct((2 * STEPS, width, CHUNK), BF16),
+            jax.ShapeDtypeStruct((SPARE + STEPS, width, CHUNK), BF16),
         ),
         in_specs=[smem(), anywhere(), anywhere(), anywhere()],
         out_specs=(anywhere(), anywhere()),

time: 85.7 us -> 87.3 us (1.019); the launches traced: 85 us -> 88.5 us
  blocking collectives: 41.9 us -> 44.8 us
    all_to_all x1, blocking collectives: 22.8 us -> 24.7 us  [local(): lax.all_to_all(parts, 'row', split_axis=0, concat_axis=0, tiled=True)]
    all_to_all x1, blocking collectives: 19.1 us -> 20.1 us  [local(): lax.all_to_all(parts, 'col', split_axis=0, concat_axis=0, tiled=True)]
where the time goes in v6:
time: 87.3 us; the launch traced here: 88.5 us
  blocking collectives  44.8 us (51%)
  Pallas kernels  25.8 us (30%)
  starting transfers between devices  16.3 us (19%)
  waiting for transfers between devices  1.53 us (2%)
    all_to_all x1, blocking collectives, local(): lax.all_to_all(parts, 'row', split_axis=0, concat_axis=0, tiled=True)  24.7 us
    all_to_all x1, blocking collectives, local(): lax.all_to_all(parts, 'col', split_axis=0, concat_axis=0, tiled=True)  20.1 us
    pallas_call x1, Pallas kernels, gather(): pl.pallas_call(gather_kernel, out_shape=(jax.ShapeDtypeStruct((SPREAD,),...  14.3 us
    ppermute x1, starting transfers between devices, local(): other = lax.ppermute(own, 'col', [(i, i ^ 1) for i in range(cols)])  8.78 us
    pallas_call x1, Pallas kernels, attend(): pl.pallas_call(functools.partial(attention_kernel, scale), out_shape=jax....  7.88 us
    all_to_all x1, starting transfers between devices, local(): lax.all_to_all(queries, 'row', split_axis=0, concat_axis=0, tiled=True)  7.52 us
    pallas_call x1, Pallas kernels, make_queries(): pl.pallas_call(query_kernel, out_shape=jax.ShapeDtypeStruct((copies, requ...  2.28 us
  transfers between devices with their start and end apart: 2, of which 1 were waited for; matrix products, arithmetic and copies ran while one was open for 0% of the time, Pallas kernels for 19%

profile of v6, /device:TPU:1, one launch (start us, length us, event | category | flops | bytes accessed | tf_op | source)
XLA Modules:
  0.0 88.5 jit_solution(11176648367445059265)
XLA Ops:
  0.0 8.8 %collective-permute-start = (bf16[576,4096]{1,0:T(8,128)(2,1)}, bf16[576,4096]{1,0:T(8,128)(2,1)}, u32[]{:S(2)}, u32[]{:S(2)}) collective-permute-start(bf16[576,4096]{1,0:T(8,128)(2,1)} %bitcast.1), channel_id=1, source_target_pairs={{0,1},{1,0},{2,3},{3,2},{4,5},{5,4},{6,7},{7,6},{8,9},{9,8},{10,11... | collective-permute-start | bytes 14155784 | tf_op jit(solution)/shard_map/ppermute | solution.py:517
  8.8 2.3 %queries.1 = bf16[32,8,1152]{2,1,0:T(8,128)(2,1)} custom-call(bf16[8,4,128]{2,1,0:T(4,128)(2,1)} %nope_any.1, bf16[8,4,64]{2,1,0:T(4,128)(2,1)} %rope_any.1, bf16[4,128,512]{2,1,0:T(8,128)(2,1)} %up_ref.1), custom_call_target="tpu_custom_call" | custom-call | tf_op jit(solution)/shard_map/queries/pallas_call | solution.py:405
  11.1 7.5 %all-to-all-start = ((bf16[32,8,1152]{2,1,0:T(8,128)(2,1)}), bf16[32,8,1152]{2,1,0:T(8,128)(2,1)S(1)}, u32[]{:S(2)}, u32[]{:S(2)}) async-start(bf16[32,8,1152]{2,1,0:T(8,128)(2,1)} %queries.1), calls=%async_computation | async-start | bytes 1179648 | tf_op jit(solution)/shard_map/all_to_all | solution.py:519
  18.6 0.0 collective-permute-done.other_ref
  18.6 14.3 %gather.1 = (s32[6291456]{0:T(1024)}, bf16[24,576,1024]{2,1,0:T(8,128)(2,1)}) custom-call(s32[8]{0:T(128)} %length_ref.1, s32[8,4096]{1,0:T(8,128)} %table_any.1, bf16[576,4096]{1,0:T(8,128)(2,1)} %bitcast.2, bf16[576,4096]{1,0:T(8,128)(2,1)} %collective-permute-done.other_ref), custom_call_target="tpu_custom_call" | custom-call | flops 10000000 | bytes 20000000 | tf_op jit(solution)/shard_map/gather/pallas_call | solution.py:425
  32.9 1.5 %all-to-all-done.query_any = bf16[32,8,1152]{2,1,0:T(8,128)(2,1)S(1)} async-done(((bf16[32,8,1152]{2,1,0:T(8,128)(2,1)}), bf16[32,8,1152]{2,1,0:T(8,128)(2,1)S(1)}, u32[]{:S(2)}, u32[]{:S(2)}) %all-to-all-start) | async-done | bytes 589856 | tf_op jit(solution)/shard_map/all_to_all | solution.py:519
  34.5 0.0 copy-start
  34.5 7.9 %attention.1 = bf16[32,8,1152]{2,1,0:T(8,128)(2,1)S(1)} custom-call(s32[6291456]{0:T(1024)} %get-tuple-element.7.plan_any, bf16[32,8,1152]{2,1,0:T(8,128)(2,1)S(1)} %all-to-all-done.query_any, bf16[24,576,1024]{2,1,0:T(8,128)(2,1)} %get-tuple-element.8.keys_any), custom_call_target="tpu_custom_call" | custom-call | flops 1200000000 | bytes 12000000 | tf_op jit(solution)/shard_map/attention/pallas_call | solution.py:460
  42.3 24.7 %all_to_all.15.part_ref = bf16[32,8,1152]{2,1,0:T(8,128)(2,1)S(1)} all-to-all(bf16[32,8,1152]{2,1,0:T(8,128)(2,1)S(1)} %attention.1), channel_id=1, replica_groups=mesh['row'=32,'col'=16] {'row'}, dimensions={0} | all-to-all | bytes 1179648 | tf_op jit(solution)/shard_map/all_to_all | solution.py:522
  67.0 0.0 copy-done
  67.1 0.5 fold.1
  67.6 20.1 %all_to_all.16.part_ref = bf16[16,8,384]{2,1,0:T(8,128)(2,1)S(1)} all-to-all(bf16[16,8,384]{2,1,0:T(8,128)(2,1)S(1)} %fold.1), channel_id=1, replica_groups=mesh['row'=32,'col'=16] {'col'}, dimensions={0} | all-to-all | bytes 196608 | tf_op jit(solution)/shard_map/all_to_all | solution.py:524
  87.7 0.8 merge.1
Async XLA Ops:
  0.0 18.6 %collective-permute-start = (bf16[576,4096]{1,0:T(8,128)(2,1)}, bf16[576,4096]{1,0:T(8,128)(2,1)}, u32[]{:S(2)}, u32[]{:S(2)}) collective-permute-start(bf16[576,4096]{1,0:T(8,128)(2,1)} %bitcast.1), channel_id=1, source_target_pairs={{0,1},{1,0},{2,3},{3,2},{4,5},{5,4},{6,7},{7,6},{8,9},{9,8},{10,11... | collective-permute-start | bytes 14155784 | tf_op jit(solution)/shard_map/ppermute | solution.py:517
  11.1 23.4 %all-to-all-start = ((bf16[32,8,1152]{2,1,0:T(8,128)(2,1)}), bf16[32,8,1152]{2,1,0:T(8,128)(2,1)S(1)}, u32[]{:S(2)}, u32[]{:S(2)}) async-start(bf16[32,8,1152]{2,1,0:T(8,128)(2,1)} %queries.1), calls=%async_computation | async-start | bytes 1179648 | tf_op jit(solution)/shard_map/all_to_all | solution.py:519
  34.5 32.6 %copy-start = (bf16[4,512,128]{2,1,0:T(8,128)(2,1)S(1)}, bf16[4,512,128]{2,1,0:T(8,128)(2,1)}, u32[]{:S(2)}) copy-start(bf16[4,512,128]{2,1,0:T(8,128)(2,1)} %up_any.1) | copy-start | bytes 1572868

commit v7 on v5

--- a/solution.py
+++ b/solution.py
@@ -277,10 +277,12 @@
     def keys(step, u, depth):
         return keys_ref[step, :depth, 2 * LANES * u : 2 * LANES * (u + 1)]
 
-    @pl.loop(0, steps)
-    def _(step):
+    whole = (groups + 1) // UNROLL
+    left_over = whole * UNROLL < groups
+
+    def score_step(step, count):
         chunk(step).wait()
-        for u in range(UNROLL):
+        for u in range(count):
             g = step * UNROLL + u
             r = plan_ref[8 + g]
             score = jnp.dot(query[r], keys(step, u, keys_ref.shape[1]), preferred_element_type=F32)
@@ -297,6 +299,14 @@
                 halves.append(part)
             top[r] = jnp.maximum(top[r], jnp.maximum(*halves))
 
+    @pl.loop(0, whole)
+    def _(step):
+        score_step(step, UNROLL)
+
+    @pl.when(left_over)
+    def _():
+        score_step(whole, 2)
+
     @pl.loop(jnp.minimum(steps, EARLY), EARLY)
     def _(step):
         chunk(step).wait()
@@ -304,9 +314,8 @@
     for r in range(requests):
         top[r] = jnp.broadcast_to(jnp.max(top[r], axis=1, keepdims=True), top.shape[1:])
 
-    @pl.loop(0, steps)
-    def _(step):
-        for u in range(UNROLL):
+    def value_step(step, count):
+        for u in range(count):
             g = step * UNROLL + u
             r = plan_ref[8 + g]
             level = top[r]
@@ -322,6 +331,14 @@
                 (((1,), (1,)), ((), ())),
                 preferred_element_type=F32,
             )
+
+    @pl.loop(0, whole)
+    def _(step):
+        value_step(step, UNROLL)
+
+    @pl.when(left_over)
+    def _():
+        value_step(whole, 2)
 
     for r in range(requests):
         sums = jnp.sum(denom[r], axis=1, keepdims=True)

time: 85.7 us -> 89.2 us (1.041)
  blocking collectives: 41.9 us -> 45.2 us
  Pallas kernels: 25.2 us -> 26.7 us
  waiting for transfers between devices: 1.55 us -> 0.59 us
    all_to_all x1, blocking collectives: 22.8 us -> 25.8 us  [local(): lax.all_to_all(parts, 'row', split_axis=0, concat_axis=0, tiled=True)]
    all_to_all x1, waiting for transfers between devices: 1.55 us -> 0.59 us  [local(): lax.all_to_all(queries, 'row', split_axis=0, concat_axis=0, tiled=True)]
    pallas_call x1, Pallas kernels: 14.3 us -> 15.2 us  [gather(): pl.pallas_call(gather_kernel, out_shape=(jax.ShapeDtypeStruct((SPREAD,),...]
  transfers between devices with their start and end apart: 2 -> 2, of which waited for: 1 -> 1; matrix products, arithmetic and copies ran while one was open for 0% -> 0% of each run, Pallas kernels for 19% -> 20%
where the time goes in v7:
time: 89.2 us; the launch traced here: 88.9 us
  blocking collectives  45.2 us (51%)
  Pallas kernels  26.7 us (30%)
  starting transfers between devices  16.3 us (18%)
    all_to_all x1, blocking collectives, local(): lax.all_to_all(parts, 'row', split_axis=0, concat_axis=0, tiled=True)  25.8 us
    all_to_all x1, blocking collectives, local(): lax.all_to_all(parts, 'col', split_axis=0, concat_axis=0, tiled=True)  19.4 us
    pallas_call x1, Pallas kernels, gather(): pl.pallas_call(gather_kernel, out_shape=(jax.ShapeDtypeStruct((SPREAD,),...  15.2 us
    ppermute x1, starting transfers between devices, local(): other = lax.ppermute(own, 'col', [(i, i ^ 1) for i in range(cols)])  8.78 us
    pallas_call x1, Pallas kernels, attend(): pl.pallas_call(functools.partial(attention_kernel, scale), out_shape=jax....  7.86 us
    all_to_all x1, starting transfers between devices, local(): lax.all_to_all(queries, 'row', split_axis=0, concat_axis=0, tiled=True)  7.52 us
    pallas_call x1, Pallas kernels, make_queries(): pl.pallas_call(query_kernel, out_shape=jax.ShapeDtypeStruct((copies, requ...  2.26 us
  transfers between devices with their start and end apart: 2, of which 1 were waited for; matrix products, arithmetic and copies ran while one was open for 0% of the time, Pallas kernels for 20%

profile of v7, /device:TPU:1, one launch (start us, length us, event | category | flops | bytes accessed | tf_op | source)
XLA Modules:
  0.0 88.9 jit_solution(17632809211557011304)
XLA Ops:
  0.0 8.8 %collective-permute-start = (bf16[576,4096]{1,0:T(8,128)(2,1)}, bf16[576,4096]{1,0:T(8,128)(2,1)}, u32[]{:S(2)}, u32[]{:S(2)}) collective-permute-start(bf16[576,4096]{1,0:T(8,128)(2,1)} %bitcast.1), channel_id=1, source_target_pairs={{0,1},{1,0},{2,3},{3,2},{4,5},{5,4},{6,7},{7,6},{8,9},{9,8},{10,11... | collective-permute-start | bytes 14155784 | tf_op jit(solution)/shard_map/ppermute | solution.py:532
  8.8 2.3 %queries.1 = bf16[32,8,1152]{2,1,0:T(8,128)(2,1)} custom-call(bf16[8,4,128]{2,1,0:T(4,128)(2,1)} %nope_any.1, bf16[8,4,64]{2,1,0:T(4,128)(2,1)} %rope_any.1, bf16[4,128,512]{2,1,0:T(8,128)(2,1)} %up_ref.1), custom_call_target="tpu_custom_call" | custom-call | tf_op jit(solution)/shard_map/queries/pallas_call | solution.py:420
  11.1 7.5 %all-to-all-start = ((bf16[32,8,1152]{2,1,0:T(8,128)(2,1)}), bf16[32,8,1152]{2,1,0:T(8,128)(2,1)S(1)}, u32[]{:S(2)}, u32[]{:S(2)}) async-start(bf16[32,8,1152]{2,1,0:T(8,128)(2,1)} %queries.1), calls=%async_computation | async-start | bytes 1179648 | tf_op jit(solution)/shard_map/all_to_all | solution.py:534
  18.6 0.0 collective-permute-done.other_ref
  18.6 15.2 %gather.1 = (s32[6291456]{0:T(1024)}, bf16[20,576,1024]{2,1,0:T(8,128)(2,1)}) custom-call(s32[8]{0:T(128)} %length_ref.1, s32[8,4096]{1,0:T(8,128)} %table_any.1, bf16[576,4096]{1,0:T(8,128)(2,1)} %bitcast.2, bf16[576,4096]{1,0:T(8,128)(2,1)} %collective-permute-done.other_ref), custom_call_target="tpu_custom_call" | custom-call | flops 10000000 | bytes 20000000 | tf_op jit(solution)/shard_map/gather/pallas_call | solution.py:440
  33.8 0.6 all-to-all-done.query_any
  34.4 0.0 copy-start
  34.4 7.9 %attention.1 = bf16[32,8,1152]{2,1,0:T(8,128)(2,1)S(1)} custom-call(s32[6291456]{0:T(1024)} %get-tuple-element.7.plan_any, bf16[32,8,1152]{2,1,0:T(8,128)(2,1)S(1)} %all-to-all-done.query_any, bf16[20,576,1024]{2,1,0:T(8,128)(2,1)} %get-tuple-element.8.keys_any), custom_call_target="tpu_custom_call" | custom-call | flops 1200000000 | bytes 12000000 | tf_op jit(solution)/shard_map/attention/pallas_call | solution.py:475
  42.3 25.8 %all_to_all.15.part_ref = bf16[32,8,1152]{2,1,0:T(8,128)(2,1)S(1)} all-to-all(bf16[32,8,1152]{2,1,0:T(8,128)(2,1)S(1)} %attention.1), channel_id=1, replica_groups=mesh['row'=32,'col'=16] {'row'}, dimensions={0} | all-to-all | bytes 1179648 | tf_op jit(solution)/shard_map/all_to_all | solution.py:537
  68.1 0.0 copy-done
  68.1 0.5 fold.1
  68.7 19.4 %all_to_all.16.part_ref = bf16[16,8,384]{2,1,0:T(8,128)(2,1)S(1)} all-to-all(bf16[16,8,384]{2,1,0:T(8,128)(2,1)S(1)} %fold.1), channel_id=1, replica_groups=mesh['row'=32,'col'=16] {'col'}, dimensions={0} | all-to-all | bytes 196608 | tf_op jit(solution)/shard_map/all_to_all | solution.py:539
  88.0 0.8 merge.1
Async XLA Ops:
  0.0 18.6 %collective-permute-start = (bf16[576,4096]{1,0:T(8,128)(2,1)}, bf16[576,4096]{1,0:T(8,128)(2,1)}, u32[]{:S(2)}, u32[]{:S(2)}) collective-permute-start(bf16[576,4096]{1,0:T(8,128)(2,1)} %bitcast.1), channel_id=1, source_target_pairs={{0,1},{1,0},{2,3},{3,2},{4,5},{5,4},{6,7},{7,6},{8,9},{9,8},{10,11... | collective-permute-start | bytes 14155784 | tf_op jit(solution)/shard_map/ppermute | solution.py:532
  11.1 23.4 %all-to-all-start = ((bf16[32,8,1152]{2,1,0:T(8,128)(2,1)}), bf16[32,8,1152]{2,1,0:T(8,128)(2,1)S(1)}, u32[]{:S(2)}, u32[]{:S(2)}) async-start(bf16[32,8,1152]{2,1,0:T(8,128)(2,1)} %queries.1), calls=%async_computation | async-start | bytes 1179648 | tf_op jit(solution)/shard_map/all_to_all | solution.py:534
  34.4 33.7 %copy-start = (bf16[4,512,128]{2,1,0:T(8,128)(2,1)S(1)}, bf16[4,512,128]{2,1,0:T(8,128)(2,1)}, u32[]{:S(2)}) copy-start(bf16[4,512,128]{2,1,0:T(8,128)(2,1)} %up_any.1) | copy-start | bytes 1572868

commit v8 on v5

--- a/solution.py
+++ b/solution.py
@@ -231,10 +231,8 @@
 
 
 def attention_kernel(
-    scale, plan_any, query_any, keys_any, out_ref, plan_ref, plan_sem, query_ref, query_sem, staged, query, scores, top, denom, total, keys_ref, sems
+    scale, plan_any, query_ref, keys_any, out_ref, plan_ref, plan_sem, staged, query, scores, top, denom, total, keys_ref, sems
 ):
-    load = pltpu.make_async_copy(query_any, query_ref, query_sem)
-    load.start()
     fetch = pltpu.make_async_copy(plan_any.at[pl.ds(0, PLAN)], plan_ref, plan_sem)
     fetch.start()
 
@@ -257,7 +255,6 @@
     top[...] = jnp.full_like(top, EMPTY)
     denom[...] = jnp.zeros_like(denom)
     total[...] = jnp.zeros_like(total)
-    load.wait()
     for t in range(wide // LANES):
         columns = query_ref[:, :, t * LANES : (t + 1) * LANES]
         staged[t] = columns.astype(F32).reshape(sources * requests, LANES)
@@ -458,12 +455,10 @@
     return pl.pallas_call(
         functools.partial(attention_kernel, scale),
         out_shape=jax.ShapeDtypeStruct((sources, requests, wide), BF16),
-        in_specs=[anywhere(), anywhere(), anywhere()],
+        in_specs=[anywhere(), vmem(), anywhere()],
         out_specs=vmem(),
         scratch_shapes=[
             pltpu.SMEM((PLAN,), jnp.int32),
-            pltpu.SemaphoreType.DMA,
-            pltpu.VMEM(queries.shape, BF16),
             pltpu.SemaphoreType.DMA,
             pltpu.VMEM((wide // LANES, sources * requests, LANES), F32),
             pltpu.VMEM((requests, heads, width), BF16),

time: 85.7 us -> 86.6 us (1.011); the launches traced: 85 us -> 87.1 us
  blocking collectives: 41.9 us -> 44.1 us
    all_to_all x1, blocking collectives: 22.8 us -> 24.5 us  [local(): lax.all_to_all(parts, 'row', split_axis=0, concat_axis=0, tiled=True)]
where the time goes in v8:
time: 86.6 us; the launch traced here: 87.1 us
  blocking collectives  44.1 us (51%)
  Pallas kernels  25.1 us (29%)
  starting transfers between devices  16.3 us (19%)
  waiting for transfers between devices  1.58 us (2%)
    all_to_all x1, blocking collectives, local(): lax.all_to_all(parts, 'row', split_axis=0, concat_axis=0, tiled=True)  24.5 us
    all_to_all x1, blocking collectives, local(): lax.all_to_all(parts, 'col', split_axis=0, concat_axis=0, tiled=True)  19.6 us
    pallas_call x1, Pallas kernels, gather(): pl.pallas_call(gather_kernel, out_shape=(jax.ShapeDtypeStruct((SPREAD,),...  14.3 us
    ppermute x1, starting transfers between devices, local(): other = lax.ppermute(own, 'col', [(i, i ^ 1) for i in range(cols)])  8.78 us
    all_to_all x1, starting transfers between devices, local(): lax.all_to_all(queries, 'row', split_axis=0, concat_axis=0, tiled=True)  7.52 us
    pallas_call x1, Pallas kernels, attend(): pl.pallas_call(functools.partial(attention_kernel, scale), out_shape=jax....  7.22 us
    pallas_call x1, Pallas kernels, make_queries(): pl.pallas_call(query_kernel, out_shape=jax.ShapeDtypeStruct((copies, requ...  2.26 us
  transfers between devices with their start and end apart: 2, of which 1 were waited for; matrix products, arithmetic and copies ran while one was open for 0% of the time, Pallas kernels for 19%

profile of v8, /device:TPU:1, one launch (start us, length us, event | category | flops | bytes accessed | tf_op | source)
XLA Modules:
  0.0 87.1 jit_solution(14786583921232181145)
XLA Ops:
  0.0 8.8 %collective-permute-start = (bf16[576,4096]{1,0:T(8,128)(2,1)}, bf16[576,4096]{1,0:T(8,128)(2,1)}, u32[]{:S(2)}, u32[]{:S(2)}) collective-permute-start(bf16[576,4096]{1,0:T(8,128)(2,1)} %bitcast.1), channel_id=1, source_target_pairs={{0,1},{1,0},{2,3},{3,2},{4,5},{5,4},{6,7},{7,6},{8,9},{9,8},{10,11... | collective-permute-start | bytes 14155784 | tf_op jit(solution)/shard_map/ppermute | solution.py:510
  8.8 2.3 %queries.1 = bf16[32,8,1152]{2,1,0:T(8,128)(2,1)} custom-call(bf16[8,4,128]{2,1,0:T(4,128)(2,1)} %nope_any.1, bf16[8,4,64]{2,1,0:T(4,128)(2,1)} %rope_any.1, bf16[4,128,512]{2,1,0:T(8,128)(2,1)} %up_ref.1), custom_call_target="tpu_custom_call" | custom-call | tf_op jit(solution)/shard_map/queries/pallas_call | solution.py:400
  11.1 7.5 %all-to-all-start = ((bf16[32,8,1152]{2,1,0:T(8,128)(2,1)}), bf16[32,8,1152]{2,1,0:T(8,128)(2,1)S(1)}, u32[]{:S(2)}, u32[]{:S(2)}) async-start(bf16[32,8,1152]{2,1,0:T(8,128)(2,1)} %queries.1), calls=%async_computation | async-start | bytes 1179648 | tf_op jit(solution)/shard_map/all_to_all | solution.py:512
  18.6 0.0 collective-permute-done.other_ref
  18.6 14.3 %gather.1 = (s32[6291456]{0:T(1024)}, bf16[20,576,1024]{2,1,0:T(8,128)(2,1)}) custom-call(s32[8]{0:T(128)} %length_ref.1, s32[8,4096]{1,0:T(8,128)} %table_any.1, bf16[576,4096]{1,0:T(8,128)(2,1)} %bitcast.2, bf16[576,4096]{1,0:T(8,128)(2,1)} %collective-permute-done.other_ref), custom_call_target="tpu_custom_call" | custom-call | flops 10000000 | bytes 20000000 | tf_op jit(solution)/shard_map/gather/pallas_call | solution.py:420
  32.9 1.6 %all-to-all-done.query_ref = bf16[32,8,1152]{2,1,0:T(8,128)(2,1)S(1)} async-done(((bf16[32,8,1152]{2,1,0:T(8,128)(2,1)}), bf16[32,8,1152]{2,1,0:T(8,128)(2,1)S(1)}, u32[]{:S(2)}, u32[]{:S(2)}) %all-to-all-start) | async-done | bytes 589856 | tf_op jit(solution)/shard_map/all_to_all | solution.py:512
  34.4 0.0 copy-start
  34.4 7.2 %attention.1 = bf16[32,8,1152]{2,1,0:T(8,128)(2,1)S(1)} custom-call(s32[6291456]{0:T(1024)} %get-tuple-element.7.plan_any, bf16[32,8,1152]{2,1,0:T(8,128)(2,1)S(1)} %all-to-all-done.query_ref, bf16[20,576,1024]{2,1,0:T(8,128)(2,1)} %get-tuple-element.8.keys_any), custom_call_target="tpu_custom_call" | custom-call | flops 1200000000 | bytes 12000000 | tf_op jit(solution)/shard_map/attention/pallas_call | solution.py:455
  41.7 24.5 %all_to_all.15.part_ref = bf16[32,8,1152]{2,1,0:T(8,128)(2,1)S(1)} all-to-all(bf16[32,8,1152]{2,1,0:T(8,128)(2,1)S(1)} %attention.1), channel_id=1, replica_groups=mesh['row'=32,'col'=16] {'row'}, dimensions={0} | all-to-all | bytes 1179648 | tf_op jit(solution)/shard_map/all_to_all | solution.py:515
  66.1 0.0 copy-done
  66.1 0.5 fold.1
  66.7 19.6 %all_to_all.16.part_ref = bf16[16,8,384]{2,1,0:T(8,128)(2,1)S(1)} all-to-all(bf16[16,8,384]{2,1,0:T(8,128)(2,1)S(1)} %fold.1), channel_id=1, replica_groups=mesh['row'=32,'col'=16] {'col'}, dimensions={0} | all-to-all | bytes 196608 | tf_op jit(solution)/shard_map/all_to_all | solution.py:517
  86.3 0.8 merge.1
Async XLA Ops:
  0.0 18.6 %collective-permute-start = (bf16[576,4096]{1,0:T(8,128)(2,1)}, bf16[576,4096]{1,0:T(8,128)(2,1)}, u32[]{:S(2)}, u32[]{:S(2)}) collective-permute-start(bf16[576,4096]{1,0:T(8,128)(2,1)} %bitcast.1), channel_id=1, source_target_pairs={{0,1},{1,0},{2,3},{3,2},{4,5},{5,4},{6,7},{7,6},{8,9},{9,8},{10,11... | collective-permute-start | bytes 14155784 | tf_op jit(solution)/shard_map/ppermute | solution.py:510
  11.1 23.4 %all-to-all-start = ((bf16[32,8,1152]{2,1,0:T(8,128)(2,1)}), bf16[32,8,1152]{2,1,0:T(8,128)(2,1)S(1)}, u32[]{:S(2)}, u32[]{:S(2)}) async-start(bf16[32,8,1152]{2,1,0:T(8,128)(2,1)} %queries.1), calls=%async_computation | async-start | bytes 1179648 | tf_op jit(solution)/shard_map/all_to_all | solution.py:512
  34.4 31.7 %copy-start = (bf16[4,512,128]{2,1,0:T(8,128)(2,1)S(1)}, bf16[4,512,128]{2,1,0:T(8,128)(2,1)}, u32[]{:S(2)}) copy-start(bf16[4,512,128]{2,1,0:T(8,128)(2,1)} %up_any.1) | copy-start | bytes 1572868
